TPU v7x, 32 devices: a whole 2x2x4 slice. The times are simulated.
32 devices in a mesh: dp: 16 (over z, x, core), tensor: 2 (over y).
Axes of the slice: x: 2, y: 2, z: 4, core: 2. Of those that a mesh axis runs over, the one named last changes fastest.
Arguments:
- x_in: bfloat16 [16384, 1024], P(('dp', 'tensor')), may hold values from -6 to 6
- source: bfloat16 [16384, 1024], P(('dp', 'tensor')), may hold values from -6 to 6
- segment: int32 [16384], P(('dp', 'tensor')), may hold values from 0 to 12, as said below
- parent: int32 [16, 13], P('dp'), may hold values from 0 to 11, as said below
- norm_gain: bfloat16 [1024, 3], P('dp'), may hold values from 0.099609375 to 1.8984375
- norm_bias: bfloat16 [1024, 3], P('dp'), may hold values from -3 to 3
- self_query: bfloat16 [1024, 1024], P('dp', 'tensor'), may hold values from -0.1875 to 0.1875
- self_key: bfloat16 [1024, 1024], P('dp', 'tensor'), may hold values from -0.1875 to 0.1875
- self_value: bfloat16 [1024, 1024], P('dp', 'tensor'), may hold values from -0.1875 to 0.1875
- self_output: bfloat16 [1024, 1024], P('dp', 'tensor'), may hold values from -0.75 to 0.75
- cross_query: bfloat16 [1024, 1024], P('dp', 'tensor'), may hold values from -0.1875 to 0.1875
- cross_key: bfloat16 [1024, 1024], P('dp', 'tensor'), may hold values from -0.1875 to 0.1875
- cross_value: bfloat16 [1024, 1024], P('dp', 'tensor'), may hold values from -0.1875 to 0.1875
- cross_output: bfloat16 [1024, 1024], P('dp', 'tensor'), may hold values from -1 to 1
- ffn_up: bfloat16 [1024, 4096], P('dp', 'tensor'), may hold values from -0.1875 to 0.1875
- ffn_down: bfloat16 [1024, 4096], P('dp', 'tensor'), may hold values from -0.09375 to 0.09375
- cotangent: bfloat16 [16384, 1024], P(('dp', 'tensor')), may hold values from -6 to 6
Outputs:
- x_out: bfloat16 [16384, 1024], P(('dp', 'tensor'))
- x_grad: float32 [16384, 1024], P(('dp', 'tensor'))
- source_grad: float32 [16384, 1024], P(('dp', 'tensor'))
- norm_gain_grad: float32 [1024, 3], P('dp')
- norm_bias_grad: float32 [1024, 3], P('dp')
- self_query_grad: float32 [1024, 1024], P('dp', 'tensor')
- self_key_grad: float32 [1024, 1024], P('dp', 'tensor')
- self_value_grad: float32 [1024, 1024], P('dp', 'tensor')
- self_output_grad: float32 [1024, 1024], P('dp', 'tensor')
- cross_query_grad: float32 [1024, 1024], P('dp', 'tensor')
- cross_key_grad: float32 [1024, 1024], P('dp', 'tensor')
- cross_value_grad: float32 [1024, 1024], P('dp', 'tensor')
- cross_output_grad: float32 [1024, 1024], P('dp', 'tensor')
- ffn_up_grad: float32 [1024, 4096], P('dp', 'tensor')
- ffn_down_grad: float32 [1024, 4096], P('dp', 'tensor')
Inputs may be any that keep to these rules, and one draw needn't show every extreme that they name: Within each tree, segment ids never fall along the tokens, start with the trunk 0 on more than half of the tree's 1024 tokens, and every id holds at least one token. parent[t, 0] = 0, parent[t, b] < b for every other segment b, and parent[t, 12] = 11 in every tree.
All inputs are finite; a program needn't handle non-finite values.
Results may differ from a plain program's by a relative error of at most 0.022.
Values may be sent and summed in bfloat16 or wider, within the bound.
No kernel may reach another device: no remote copies, remote signals or barrier semaphores. Data moves between devices by JAX's collectives and lax.ppermute only.
A program may use at most 192 MiB of HBM per device.

v0:
```python
import functools

import jax
import jax.numpy as jnp
import numpy as np
from jax import lax
from jax.experimental import pallas as pl
from jax.experimental.pallas import tpu as pltpu
from jax.sharding import PartitionSpec as P

HEAD_DIM = 64
PAIR = 128
EPSILON = 1e-05
HIDDEN = -1e30
AXES = ("dp", "tensor")
BF = jnp.bfloat16
F32 = jnp.float32
VMEM_LIMIT = 50 * 2**20
KERNEL_COST = pl.CostEstimate(flops=1, bytes_accessed=1024, transcendentals=0)


def dot(former, latter, dims, kind=F32):
    return lax.dot_general(former, latter, (dims, ((), ())), preferred_element_type=kind)


def mm(former, latter, kind=F32):
    return dot(former, latter, ((1,), (0,)), kind)


def mm_lt(former, latter, kind=F32):
    return dot(former, latter, ((0,), (0,)), kind)


def mm_rt(former, latter, kind=F32):
    return dot(former, latter, ((1,), (1,)), kind)


def head_masks(values):
    lane = lax.broadcasted_iota(jnp.int32, values.shape, 1)
    zero = jnp.zeros_like(values)
    return (
        jnp.where(lane < HEAD_DIM, values, zero),
        jnp.where(lane >= HEAD_DIM, values, zero),
    )


def causal_bias(rows, columns, row_start, column_start):
    row = lax.broadcasted_iota(jnp.int32, (rows, columns), 0) + row_start
    column = lax.broadcasted_iota(jnp.int32, (rows, columns), 1) + column_start
    return row, column


def attention_kernel(tree, block, *refs):
    if tree:
        q_ref, k_ref, v_ref, qbits_ref, kbits_ref, o_ref, lse_ref, bias_ref = refs
    else:
        q_ref, k_ref, v_ref, o_ref, lse_ref = refs
    tokens = q_ref.shape[0]
    keys = k_ref.shape[0]
    half = tokens // 2
    if tree:

        @pl.when(pl.program_id(0) == 0)
        def _():
            row, column = causal_bias(half, half, 0, 0)
            seen = (qbits_ref[half:, :] & kbits_ref[:, half:]) != 0
            bias_ref[...] = jnp.where(seen & (column <= row), 0.0, HIDDEN)

    lane = lax.broadcasted_iota(jnp.int32, (block, PAIR), 1)
    for start in range(0, tokens, block):
        last = start + block if tree else keys
        queries = head_masks(q_ref[start : start + block, :] * BF(HEAD_DIM ** (-0.5)))
        key_rows = k_ref[:last, :]
        value_rows = v_ref[:last, :]
        outs = []
        sums = []
        for side in range(2):
            scores = mm_rt(queries[side], key_rows)
            if tree:
                if start < half:
                    row, column = causal_bias(block, block, 0, 0)
                    tail = scores[:, start:] + jnp.where(column <= row, 0.0, HIDDEN)
                    split = start
                else:
                    tail = (
                        scores[:, half:]
                        + bias_ref[start - half : start - half + block, : last - half]
                    )
                    split = half
                scores = tail if split == 0 else jnp.concatenate([scores[:, :split], tail], 1)
            top = jnp.max(scores, 1, keepdims=True)
            weights = jnp.exp(scores - top)
            total = jnp.sum(weights, 1, keepdims=True)
            outs.append(mm(weights.astype(BF), value_rows) * (1.0 / total))
            sums.append(top + jnp.log(total))
        o_ref[start : start + block, :] = jnp.where(lane < HEAD_DIM, outs[0], outs[1]).astype(BF)
        lse_ref[start : start + block, :] = jnp.where(lane < HEAD_DIM, sums[0], sums[1])


def attention(q, k, v, offsets, pairs, bits, block=256):
    tokens = q.shape[0]
    tree = bits is not None

    def spec(rows, shift):
        return pl.BlockSpec((rows, PAIR), lambda i, shift=shift: (0, i + shift))

    in_specs = [spec(tokens, offsets[0]), spec(k.shape[0], offsets[1]), spec(v.shape[0], offsets[2])]
    operands = [q, k, v]
    scratch = []
    if tree:
        in_specs += [
            pl.BlockSpec((tokens, 1), lambda i: (0, 0)),
            pl.BlockSpec((1, tokens), lambda i: (0, 0)),
        ]
        operands += list(bits)
        scratch = [pltpu.VMEM((tokens // 2, tokens // 2), F32)]
    return pl.pallas_call(
        functools.partial(attention_kernel, tree, block),
        grid=(pairs,),
        in_specs=in_specs,
        out_specs=[spec(tokens, 0), spec(tokens, 0)],
        out_shape=[
            jax.ShapeDtypeStruct((tokens, pairs * PAIR), BF),
            jax.ShapeDtypeStruct((tokens, pairs * PAIR), F32),
        ],
        scratch_shapes=scratch,
        compiler_params=pltpu.CompilerParams(vmem_limit_bytes=VMEM_LIMIT),
        cost_estimate=KERNEL_COST,
    )(*operands)


def attention_back_kernel(tree, block, *refs):
    if tree:
        (q_ref, k_ref, v_ref, o_ref, lse_ref, do_ref, qbits_ref, kbits_ref,
         dq_ref, dk_ref, dv_ref, dq_acc, bias_ref) = refs
    else:
        q_ref, k_ref, v_ref, o_ref, lse_ref, do_ref, dq_ref, dk_ref, dv_ref, dq_acc = refs
    tokens = q_ref.shape[0]
    keys = k_ref.shape[0]
    half = tokens // 2
    scale = HEAD_DIM ** (-0.5)
    if tree:

        @pl.when(pl.program_id(0) == 0)
        def _():
            row, column = causal_bias(half, half, 0, 0)
            seen = (kbits_ref[half:, :] & qbits_ref[:, half:]) != 0
            bias_ref[...] = jnp.where(seen & (row <= column), 0.0, HIDDEN)

    queries = head_masks(q_ref[...] * BF(scale))
    grads = head_masks(do_ref[...])
    pick_row = lax.broadcasted_iota(jnp.int32, (8, PAIR), 0)
    pick_lane = lax.broadcasted_iota(jnp.int32, (8, PAIR), 1)
    pick = ((pick_lane // HEAD_DIM) == pick_row).astype(F32)
    product = do_ref[...].astype(F32) * o_ref[...].astype(F32)
    delta = lax.dot_general(
        pick, product, (((1,), (1,)), ((), ())), precision=lax.Precision.HIGHEST,
        preferred_element_type=F32,
    )
    lse_rows = jnp.transpose(lse_ref[...])
    for start in range(0, keys, block):
        first = start if tree else 0
        key_rows = k_ref[start : start + block, :]
        key_masked = head_masks(key_rows)
        value_rows = v_ref[start : start + block, :]
        dv = None
        dk = None
        dq = None
        for side in range(2):
            stat = lse_rows[side * HEAD_DIM : side * HEAD_DIM + 1, first:]
            scores = mm_rt(key_rows, queries[side][first:, :]) - stat
            if tree:
                if start < half:
                    row, column = causal_bias(block, block, 0, 0)
                    head = scores[:, :block] + jnp.where(row <= column, 0.0, HIDDEN)
                    scores = jnp.concatenate([head, scores[:, block:]], 1)
                else:
                    scores = scores + bias_ref[start - half : start - half + block, first - half :]
            weights = jnp.exp(scores)
            dv_part = mm(weights.astype(BF), grads[side][first:, :])
            weight_grad = mm_rt(value_rows, grads[side][first:, :])
            score_grad = (weights * (weight_grad - delta[side : side + 1, first:])).astype(BF)
            dk_part = mm(score_grad, queries[side][first:, :])
            dq_part = mm_lt(score_grad, key_masked[side])
            dv = dv_part if dv is None else dv + dv_part
            dk = dk_part if dk is None else dk + dk_part
            dq = dq_part if dq is None else dq + dq_part
        dv_ref[start : start + block, :] = dv.astype(BF)
        dk_ref[start : start + block, :] = dk.astype(BF)
        if start == 0:
            dq_acc[...] = dq
        else:
            dq_acc[first:, :] += dq
    dq_ref[...] = (dq_acc[...] * scale).astype(BF)


def attention_back(q, k, v, o, lse, do, offsets, pairs, bits, block=256):
    tokens = q.shape[0]
    keys = k.shape[0]
    tree = bits is not None

    def spec(rows, shift):
        return pl.BlockSpec((rows, PAIR), lambda i, shift=shift: (0, i + shift))

    in_specs = [
        spec(tokens, offsets[0]), spec(keys, offsets[1]), spec(keys, offsets[2]),
        spec(tokens, 0), spec(tokens, 0), spec(tokens, 0),
    ]
    operands = [q, k, v, o, lse, do]
    scratch = [pltpu.VMEM((tokens, PAIR), F32)]
    if tree:
        in_specs += [
            pl.BlockSpec((1, tokens), lambda i: (0, 0)),
            pl.BlockSpec((tokens, 1), lambda i: (0, 0)),
        ]
        operands += list(bits)
        scratch.append(pltpu.VMEM((tokens // 2, tokens // 2), F32))
    return pl.pallas_call(
        functools.partial(attention_back_kernel, tree, block),
        grid=(pairs,),
        in_specs=in_specs,
        out_specs=[spec(tokens, 0), spec(keys, 0), spec(keys, 0)],
        out_shape=[
            jax.ShapeDtypeStruct((tokens, pairs * PAIR), BF),
            jax.ShapeDtypeStruct((keys, pairs * PAIR), BF),
            jax.ShapeDtypeStruct((keys, pairs * PAIR), BF),
        ],
        scratch_shapes=scratch,
        compiler_params=pltpu.CompilerParams(vmem_limit_bytes=VMEM_LIMIT),
        cost_estimate=KERNEL_COST,
    )(*operands)


class Links:
    def __init__(self, dp_size):
        self.devices = 2 * dp_size
        self.places = dp_size // 2
        self.grid = dp_size == 16

    def begin(self):
        self.place = lax.axis_index("dp") // 2
        self.core = lax.axis_index("dp") % 2
        self.side = lax.axis_index("tensor")
        self.home = self.core == self.side

    def send(self, values, pairs):
        return lax.ppermute(values, AXES, pairs)

    def quad(self, values, edges):
        pairs = [(4 * m + s, 4 * m + t) for m in range(self.places) for s, t in edges]
        return self.send(values, pairs)

    def cross_begin(self, values):
        return values, self.quad(values, [(1, 2), (2, 1)])

    def cross_end(self, pending):
        return jnp.where(self.home, *pending)

    def cross(self, values):
        return self.cross_end(self.cross_begin(values))

    def swap_cores(self, values):
        return self.quad(values, [(0, 2), (1, 3), (2, 0), (3, 1)])

    def gather(self, shard):
        return lax.all_gather(shard, "dp", axis=0, tiled=True)

    def sides_begin(self, shard):
        return self.cross_begin(shard), self.quad(shard, [(0, 1), (1, 3), (3, 2), (2, 0)])

    def gather_sides_first(self, pending):
        former, latter = self.cross_end(pending[0]), pending[1]
        first_side = self.side == 0
        both = jnp.concatenate(
            [jnp.where(first_side, former, latter), jnp.where(first_side, latter, former)], 0
        )
        groups = [[2 * m + c for m in range(self.places)] for c in range(2)]
        return lax.all_gather(both, "dp", axis=0, tiled=True, axis_index_groups=groups)

    def scatter(self, crossed):
        return lax.psum_scatter(crossed, "dp", scatter_dimension=0, tiled=True).astype(F32)

    def total(self, values, bits):
        if not self.grid:
            return lax.psum(values, AXES) if 1 in bits else values
        for bit in bits:
            values = values + self.send(values, [(i, i ^ bit) for i in range(self.devices)])
        return values


def pick(values, index, axis):
    return lax.dynamic_index_in_dim(values, index, axis, keepdims=False)


def rounded_sum(former, latter):
    return (former.astype(F32) + latter.astype(F32)).astype(BF)


def together(*values):
    return lax.optimization_barrier(values)


class Scatter:
    def __init__(self, links, first, second):
        self.links = links
        self.state = first, second

    def exchange(self, values, axis, bit, index):
        kept, sent = pick(values, index, axis), pick(values, 1 - index, axis)
        return kept, self.links.send(sent, [(i, i ^ bit) for i in range(self.links.devices)])

    def sides(self, values, axis):
        links = self.links
        former, latter = pick(values, links.side, axis), pick(values, 1 - links.side, axis)
        return links.cross_begin(former), links.quad(latter, [(1, 0), (3, 1), (2, 3), (0, 2)])

    def sides_end(self, pending):
        return rounded_sum(self.links.cross_end(pending[0]), pending[1])

    def first(self):
        links = self.links
        if not links.grid:
            whole = jnp.concatenate(self.state, 1)
            self.state = links.scatter(links.cross(whole))
            return
        former, latter = (
            part.reshape(2, 2, 2, 2, part.shape[0] // 16, part.shape[1]) for part in self.state
        )
        self.state = self.sides(former, 3), self.exchange(latter, 2, 4, links.place % 2)

    def second(self):
        links = self.links
        if links.grid:
            former, latter = self.sides_end(self.state[0]), rounded_sum(*self.state[1])
            self.state = self.exchange(former, 2, 4, links.place % 2), self.sides(latter, 2)

    def far(self):
        if self.links.grid:
            both = jnp.concatenate(
                [rounded_sum(*self.state[0]), self.sides_end(self.state[1])], -1
            )
            self.state = self.exchange(both, 0, 16, self.links.place // 4)

    def near(self):
        if self.links.grid:
            whole = rounded_sum(*self.state)
            self.state = self.exchange(whole, 0, 8, self.links.place // 2 % 2)

    def result(self):
        if self.links.grid:
            self.state = self.state[0].astype(F32) + self.state[1].astype(F32)
        return self.state

    def after(self, *values):
        self.state, values = lax.optimization_barrier((self.state, values))
        return values


def ancestor_bits(segment_all, parent_row):
    nodes = parent_row.shape[0]
    node_ids = jnp.arange(nodes, dtype=jnp.int32)
    current = node_ids
    seen = jnp.zeros((nodes,), jnp.int32)
    for _ in range(nodes):
        seen = seen | jnp.left_shift(1, current)
        current = jnp.sum(jnp.where(current[:, None] == node_ids[None, :], parent_row[None, :], 0), 1)
    query_bits = jnp.sum(
        jnp.where(segment_all[:, None] == node_ids[None, :], seen[None, :], 0), 1
    )
    return query_bits, jnp.left_shift(1, segment_all)


def norm_stats(values):
    mean = jnp.mean(values, -1, keepdims=True)
    centered = values - mean
    variance = jnp.mean(centered * centered, -1, keepdims=True)
    return centered, lax.rsqrt(variance + EPSILON)


def norm(values, gain_row, offset):
    centered, inverse = norm_stats(values)
    return centered * inverse * gain_row + offset


def norm_back(values, gain_row, grad):
    centered, inverse = norm_stats(values)
    normed = centered * inverse
    scaled = grad * gain_row
    back = inverse * (
        scaled
        - jnp.mean(scaled, -1, keepdims=True)
        - normed * jnp.mean(scaled * normed, -1, keepdims=True)
    )
    return back, grad * normed


def shards(
    links,
    x_in,
    source,
    segment,
    parent,
    norm_gain,
    norm_bias,
    self_query,
    self_key,
    self_value,
    self_output,
    cross_query,
    cross_key,
    cross_value,
    cross_output,
    ffn_up,
    ffn_down,
    cotangent,
):
    half, width = x_in.shape
    tokens = 2 * half
    rows = self_query.shape[0]
    heads_width = self_query.shape[1]
    hidden = ffn_up.shape[1]
    pairs = heads_width // PAIR
    links.begin()
    first_core = links.core == 0

    def both_halves(mine):
        other = links.swap_cores(mine)
        return jnp.concatenate(
            [jnp.where(first_core, mine, other), jnp.where(first_core, other, mine)], 0
        )

    def my_half(values):
        return jnp.where(first_core, values[:half], values[half:])

    def other_half(values):
        return jnp.where(first_core, values[half:], values[:half])

    def joined(part):
        return part.astype(F32) + links.swap_cores(part).astype(F32)

    def joined_half(part):
        return my_half(part).astype(F32) + links.swap_cores(other_half(part)).astype(F32)

    nodes = parent.shape[1]
    labels = jnp.concatenate(
        [segment, parent[0], jnp.zeros((PAIR - nodes,), jnp.int32)]
    ).reshape(-1, PAIR)
    segment_rows = half // PAIR
    pad = PAIR - norm_gain.shape[1] - norm_bias.shape[1]
    norms_shard = jnp.concatenate(
        [norm_gain, norm_bias, jnp.zeros((rows, pad), BF)], 1
    )
    two, three, four = 2 * heads_width, 3 * heads_width, 4 * heads_width
    self_w = links.gather(
        jnp.concatenate([self_query, self_key, self_value, self_output, norms_shard], 1)
    )
    cross_w = links.gather(
        jnp.concatenate([cross_query, cross_key, cross_value, cross_output], 1)
    )
    up_w = links.gather(ffn_up)
    moved = links.cross_begin(labels), links.cross_begin(x_in)
    others = links.cross_begin(jnp.concatenate([source, cotangent], 0))
    down_w = links.sides_begin(ffn_down)
    self_w, moved, others, down_w = together(self_w, moved, others, down_w)
    down_w = links.gather_sides_first(down_w)
    self_w = links.cross_begin(self_w)
    labels, x_mine = links.cross_end(moved[0]), links.cross_end(moved[1])
    others = links.cross_end(others)
    x_zero = both_halves(x_mine).astype(F32)
    segment_all = both_halves(labels[:segment_rows]).reshape(tokens)
    query_bits, key_bits = ancestor_bits(segment_all, labels[segment_rows, :nodes])
    forward_bits = (query_bits[:, None], key_bits[None, :])
    backward_bits = (query_bits[None, :], key_bits[:, None])
    source_all = both_halves(others[:half])
    grad_top = both_halves(others[half:])
    centered, inverse = norm_stats(x_zero)
    normed = centered * inverse
    self_w, normed, source_all, grad_top = together(self_w, normed, source_all, grad_top)
    self_w = links.cross_end(self_w)
    norms = self_w[:, four : four + 8].astype(F32).T
    gain = [norms[i : i + 1] for i in range(3)]
    shift = [norms[i + 3 : i + 4] for i in range(3)]

    hidden_one = (normed * gain[0] + shift[0]).astype(BF)
    hidden_one, cross_w = together(hidden_one, cross_w)
    cross_w = links.cross_begin(cross_w)
    qkv = mm(hidden_one, self_w[:, :three], BF)
    self_places = (0, pairs, 2 * pairs)
    mixed_one, lse_one = attention(qkv, qkv, qkv, self_places, pairs, forward_bits)
    x_one = x_zero + joined(mm_rt(mixed_one, self_w[:, three:four], BF))
    hidden_two = norm(x_one, gain[1], shift[1]).astype(BF)
    hidden_two, up_w = together(hidden_two, up_w)
    up_w = links.cross_begin(up_w)
    cross_w = links.cross_end(cross_w)
    cross_queries = mm(hidden_two, cross_w[:, :heads_width], BF)
    memory = mm(source_all, cross_w[:, heads_width:three], BF)
    cross_places = (0, 0, pairs)
    mixed_two, lse_two = attention(cross_queries, memory, memory, cross_places, pairs, None)
    x_two = x_one + joined(mm_rt(mixed_two, cross_w[:, three:four], BF))
    hidden_three = norm(x_two, gain[2], shift[2]).astype(BF)
    hidden_three, up_w = together(hidden_three, up_w)
    up_w = links.cross_end(up_w)
    active = mm(hidden_three, up_w)
    normal = 0.5 * (1.0 + lax.erf(active * np.float32(0.5**0.5)))
    slope = (
        normal + active * jnp.exp(-0.5 * active * active) * np.float32((2.0 * np.pi) ** -0.5)
    ).astype(BF)
    activated = (active * normal).astype(BF)
    down_grad = mm_lt(grad_top, activated, BF)
    down_w, down_grad, activated, slope = together(down_w, down_grad, activated, slope)

    def norm_sums(values, grad):
        return jnp.sum(my_half(values), 0), jnp.sum(my_half(grad), 0)

    down_grad = links.cross_begin(down_grad)
    active_grad = (mm(grad_top, down_w) * slope.astype(F32)).astype(BF)
    up_grad = links.cross_begin(mm_lt(hidden_three, active_grad, BF))
    out_part = mm_rt(activated, down_w, BF)
    normed_grad = joined(mm_rt(active_grad, up_w, BF))
    back, gain_part = norm_back(x_two, gain[2], normed_grad)
    gain_three, shift_three = norm_sums(gain_part, normed_grad)
    grad_two = grad_top.astype(F32) + back
    grad_two_low = grad_two.astype(BF)
    mixed_grad = mm(grad_two_low, cross_w[:, three:four], BF)
    dq, dk, dv = attention_back(
        cross_queries, memory, memory, mixed_two, lse_two, mixed_grad, cross_places, pairs, None
    )
    dq, dk, dv, down_grad = together(dq, dk, dv, down_grad)
    down_grad = links.scatter(links.cross_end(down_grad))
    part = mm_rt(dq, cross_w[:, :heads_width], BF)
    normed_grad = joined(part)
    dkv = jnp.concatenate([dk, dv], 1)
    cross_grad = Scatter(
        links,
        jnp.concatenate([mm_lt(hidden_two, dq, BF), mm_lt(grad_two_low, mixed_two, BF)], 1),
        mm_lt(source_all, dkv, BF),
    )
    cross_grad.first()
    back, gain_part = norm_back(x_one, gain[1], normed_grad)
    gain_two, shift_two = norm_sums(gain_part, normed_grad)
    grad_one = grad_two + back
    grad_one_low = grad_one.astype(BF)
    mixed_grad = mm(grad_one_low, self_w[:, three:four], BF)
    mixed_grad, up_grad = cross_grad.after(mixed_grad, up_grad)
    cross_grad.second()
    up_grad = links.scatter(links.cross_end(up_grad))
    x_three = (my_half(x_two) + joined_half(out_part)).astype(BF)
    source_part = joined_half(mm_rt(dkv, cross_w[:, heads_width:three], BF)).astype(BF)
    outs = links.cross_begin(jnp.concatenate([x_three, source_part], 0))
    dq, dk, dv = attention_back(
        qkv, qkv, qkv, mixed_one, lse_one, mixed_grad, self_places, pairs, backward_bits
    )
    dq, dk, dv = cross_grad.after(dq, dk, dv)
    cross_grad.far()
    dqkv = jnp.concatenate([dq, dk, dv], 1)
    qkv_grad = mm_lt(hidden_one, dqkv, BF)
    self_grad = Scatter(
        links,
        qkv_grad[:, :two],
        jnp.concatenate([qkv_grad[:, two:], mm_lt(grad_one_low, mixed_one, BF)], 1),
    )
    self_grad.first()
    normed_grad = joined_half(mm_rt(dqkv, self_w[:, :three], BF))
    back, gain_part = norm_back(my_half(x_zero), gain[0], normed_grad)
    gain_one, shift_one = jnp.sum(gain_part, 0), jnp.sum(normed_grad, 0)
    x_grad_mine = (my_half(grad_one) + back).astype(BF)
    sums = jnp.stack(
        [gain_one, gain_two, gain_three, shift_one, shift_two, shift_three,
         jnp.zeros_like(gain_one), jnp.zeros_like(gain_one)]
    )
    sums = links.total(sums, (2, 8))
    x_grad_mine, sums = self_grad.after(x_grad_mine, sums)
    self_grad.second()
    cross_grad.near()
    sums = links.total(sums, (16,))
    outs, sums, cross_grad.state = self_grad.after(outs, sums, cross_grad.state)
    self_grad.far()
    cross_grad = cross_grad.result()
    x_grad = links.cross_begin(x_grad_mine)
    sums = links.total(sums, (4, 1))
    outs = links.cross_end(outs)
    x_out = outs[:half]
    source_grad = outs[half:].astype(F32)
    x_grad, sums, cross_grad, x_out, source_grad = self_grad.after(
        x_grad, sums, cross_grad, x_out, source_grad
    )
    self_grad.near()
    x_grad = links.cross_end(x_grad).astype(F32)
    norm_mine = lax.dynamic_slice(sums, (0, lax.axis_index("dp") * rows), (8, rows)).T
    self_grad = self_grad.result()

    def piece(values, number):
        return values[:, number * heads_width : (number + 1) * heads_width]

    return (
        x_out,
        x_grad,
        source_grad,
        norm_mine[:, :3],
        norm_mine[:, 3:6],
        piece(self_grad, 0),
        piece(self_grad, 1),
        piece(self_grad, 2),
        piece(self_grad, 3),
        piece(cross_grad, 0),
        piece(cross_grad, 2),
        piece(cross_grad, 3),
        piece(cross_grad, 1),
        up_grad,
        down_grad,
    )


def solution(mesh):
    rows = P(AXES, None)
    split = P("dp", "tensor")
    narrow = P("dp", None)
    placed = (rows, rows, P(AXES), narrow, narrow, narrow) + (split,) * 10 + (rows,)
    return jax.shard_map(
        functools.partial(shards, Links(mesh.shape["dp"])),
        mesh=mesh,
        in_specs=placed,
        out_specs=(rows, rows, rows, narrow, narrow) + (split,) * 10,
        check_vma=False,
    )
```

profile of v0, /device:TPU:0, one launch (start us, length us, event | category | flops | bytes accessed | tf_op | source)
XLA Modules:
  0.0 563.4 jit_solution(18162535102644183789)
XLA Ops:
  24.3 5.5 collective-permute-start.4
  30.6 5.9 %collective-permute-done.4 = bf16[64,2048]{1,0:T(8,128)(2,1)} collective-permute-done((bf16[64,2048]{1,0:T(8,128)(2,1)S(1)}, bf16[64,2048]{1,0:T(8,128)(2,1)}, u32[]{:S(2)}, u32[]{:S(2)}) %collective-permute-start.4) | collective-permute-done | bytes 262176 | tf_op jit(solution)/shard_map/ppermute | solution.py:247
  36.6 29.0 %all-gather.5.cloned.1.call-done = bf16[1024,2176]{1,0:T(8,128)(2,1)} async-done(((bf16[64,2176]{1,0:T(8,128)(2,1)}), bf16[1024,2176]{1,0:T(8,128)(2,1)}) %all-gather.5.cloned.1.call-update) | async-done | bytes 4456464 | tf_op jit(solution)/shard_map/all_gather | solution.py:266
  93.8 23.7 %all-gather.7.cloned.1.call-done = bf16[1024,2048]{1,0:T(8,128)(2,1)} async-done(((bf16[64,2048]{1,0:T(8,128)(2,1)}), bf16[1024,2048]{1,0:T(8,128)(2,1)}) %all-gather.7.cloned.1.call-update) | async-done | bytes 4194320 | tf_op jit(solution)/shard_map/all_gather | solution.py:266
  117.4 2.9 collective-permute-start.11
  120.4 7.6 %fusion.7.refs_0_.refs_1_.refs_2_ = bf16[1024,1536]{1,0:T(8,128)(2,1)} fusion(bf16[1024,1024]{0,1:T(8,128)(2,1)} %add_convert_fusion.2, bf16[1024,2176]{1,0:T(8,128)(2,1)} %copy-done.26), kind=kOutput, calls=%fused_computation.36 | convolution fusion | flops 3221225472 | bytes 8388608 | tf_op jit(solution)/shard_map/dot_general | solution.py:23
  128.0 15.0 %shard_map.280 = (bf16[1024,512]{1,0:T(8,128)(2,1)S(1)}, f32[1024,512]{1,0:T(8,128)S(1)}) custom-call(bf16[1024,1536]{1,0:T(8,128)(2,1)} %fusion.7.refs_0_.refs_1_.refs_2_, bf16[1024,1536]{1,0:T(8,128)(2,1)} %fusion.7.refs_0_.refs_1_.refs_2_, bf16[1024,1536]{1,0:T(8,128)(2,1)} %fusion.7.refs_0_.refs_1_.refs_2_, s32[1024,1]{1,0:T(8,128)S(1)} %copy.87.refs_3_, ...), custom_call_target="tpu_custom_call" | custom-call | flops 1 | bytes 1024 | tf_op jit(solution)/shard_map/pallas_call | solution.py:117
  143.0 4.7 fusion.45
  147.7 13.8 %collective-permute-start.10 = (bf16[1024,1024]{0,1:T(8,128)(2,1)}, bf16[1024,1024]{0,1:T(8,128)(2,1)}, u32[]{:S(2)}, u32[]{:S(2)}) collective-permute-start(bf16[1024,1024]{0,1:T(8,128)(2,1)} %fusion.45), channel_id=1, source_target_pairs={{0,2},{1,3},{2,0},{3,1},{4,6},{5,7},{6,4},{7,5},{8,10},{9,11},{10,... | collective-permute-start | bytes 6291464 | tf_op jit(solution)/shard_map/ppermute | solution.py:247
  165.6 3.6 fusion.61
  173.2 3.3 collective-permute-start.13
  176.5 2.9 broadcast_select_fusion.4
  179.4 3.7 fusion.23.refs_1_.refs_2_
  184.4 19.1 %shard_map.281 = (bf16[1024,512]{1,0:T(8,128)(2,1)S(1)}, f32[1024,512]{1,0:T(8,128)}) custom-call(bf16[1024,512]{1,0:T(8,128)(2,1)S(1)} %fusion.42.refs_0_, bf16[1024,1024]{1,0:T(8,128)(2,1)} %fusion.23.refs_1_.refs_2_, bf16[1024,1024]{1,0:T(8,128)(2,1)} %fusion.23.refs_1_.refs_2_), custom_call_target="tpu_custom_call" | custom-call | flops 1 | bytes 1024 | tf_op jit(solution)/shard_map/pallas_call | solution.py:117
  206.1 4.1 collective-permute-start.12
  214.3 3.6 fusion.60
  222.4 9.4 %fusion.4 = (bf16[1024,2048]{1,0:T(8,128)(2,1)}, bf16[1024,2048]{1,0:T(8,128)(2,1)S(1)}) fusion(bf16[1024,1024]{0,1:T(8,128)(2,1)S(1)} %add_convert_fusion, bf16[1024,2048]{1,0:T(8,128)(2,1)S(1)} %copy-done.56, bf16[1024,2048]{1,0:T(8,128)(2,1)} %collective-permute-done.13, pred[]{:T(512)S(6)} %eq.94), kind=kOutput, calls=%fused_computation.5 | convolution fusion | flops 4320133120 | bytes 18874368 | tf_op jit(solution)/shard_map/dot_general | solution.py:23
  233.8 6.1 %fusion.65 = bf16[1024,2048]{1,0:T(8,128)(2,1)} fusion(bf16[1024,1024]{0,1:T(8,128)(2,1)S(1)} %copy-done.23, bf16[1024,2048]{1,0:T(8,128)(2,1)S(1)} %get-tuple-element.149), kind=kOutput, calls=%fused_computation.233 | convolution fusion | flops 4294967296 | bytes 10485760 | tf_op jit(solution)/shard_map/dot_general | solution.py:23
  239.9 3.4 all-gather.11.cloned.1.call-done
  243.3 7.8 %multiply_convert_fusion = bf16[1024,2048]{1,0:T(8,128)(2,1)S(1)} fusion(bf16[1024,2048]{1,0:T(8,128)(2,1)} %get-tuple-element.123, bf16[1024,1024]{0,1:T(8,128)(2,1)S(1)} %copy-done.23, bf16[1024,2048]{1,0:T(8,128)(2,1)} %all-gather.11.cloned.1.call-done), kind=kOutput, calls=%fused_computation.6 | convolution fusion | flops 4301258752 | bytes 14680064 | tf_op jit(solution)/shard_map/dot_general | solution.py:23
  251.2 4.8 fusion.26
  256.0 4.2 collective-permute-start.14
  260.2 5.2 fusion.70
  268.4 6.1 %fusion.68 = bf16[1024,2048]{1,0:T(8,128)(2,1)} fusion(bf16[1024,1024]{0,1:T(8,128)(2,1)S(1)} %copy-done.37, bf16[1024,2048]{1,0:T(8,128)(2,1)S(1)} %multiply_convert_fusion), kind=kOutput, calls=%fused_computation.236 | convolution fusion | flops 4294967296 | bytes 10485760 | tf_op jit(solution)/shard_map/dot_general | solution.py:23
  281.1 3.7 convert_add_fusion.1
  284.8 4.3 fusion.35.refs_5_
  289.1 27.8 %shard_map.282 = (bf16[1024,512]{1,0:T(8,128)(2,1)S(1)}, bf16[1024,512]{1,0:T(8,128)(2,1)S(1)}, bf16[1024,512]{1,0:T(8,128)(2,1)S(1)}) custom-call(bf16[1024,512]{1,0:T(8,128)(2,1)} %copy-done, bf16[1024,1024]{1,0:T(8,128)(2,1)} %fusion.23.refs_1_.refs_2_, bf16[1024,1024]{1,0:T(8,128)(2,1)} %fusion.23.refs_1_.refs_2_, bf16[1024,512]{1,0:T(8,128)(2,1)} %copy-done.2, ...), custom_call_target="tpu_custom_call" | custom-call | flops 1 | bytes 1024 | tf_op jit(solution)/shard_map/pallas_call | solution.py:218
  322.1 3.7 fusion.21
  329.5 4.6 broadcast_select_fusion.1
  336.8 3.0 fusion.66
  341.4 2.9 copy.90
  344.3 4.8 fusion.67
  357.1 3.6 multiply_reduce_fusion.5
  360.7 6.3 %fusion.9 = (f32[1024,1024]{0,1:T(8,128)}, f32[1024,1024]{0,1:T(8,128)S(1)}, f32[1024,1024]{0,1:T(8,128)}) fusion(f32[1024,1024]{0,1:T(8,128)S(1)} %copy-done.12, f32[1024]{0:T(1024)S(1)} %add_rsqrt_fusion.1, f32[1024]{0:T(1024)S(1)} %broadcast_multiply_fusion.5, bf16[1024,1024]{0,1:T(8,128)(2,1)} %collective-permute-done.19, bf16[1024,1024]{0,1:T(8,128)(2,1)} %fusion.40, ...), kind=kLoop, calls=%fused_computation.38 | loop fusion | flops 12582912 | bytes 25186304 | tf_op jit(solution)/shard_map/mul | solution.py:394
  367.0 4.3 fusion.31.refs_5_
  371.3 13.3 %collective-permute-done.18 = bf16[2,2,2,64,1024]{4,3,2,1,0:T(8,128)(2,1)S(1)} collective-permute-done((bf16[2,2,2,64,1024]{4,3,2,1,0:T(8,128)(2,1)S(1)}, bf16[2,2,2,64,1024]{4,3,2,1,0:T(8,128)(2,1)S(1)}, u32[]{:S(2)}, u32[]{:S(2)}) %collective-permute-start.18) | collective-permute-done | bytes 1048608 | tf_op jit(solution)/shard_map/ppermute | solution.py:247
  389.5 4.7 broadcast_select_fusion.2
  394.2 4.0 fusion.14
  398.9 20.4 %shard_map.283 = (bf16[1024,512]{1,0:T(8,128)(2,1)S(1)}, bf16[1024,512]{1,0:T(8,128)(2,1)S(1)}, bf16[1024,512]{1,0:T(8,128)(2,1)S(1)}) custom-call(bf16[1024,1536]{1,0:T(8,128)(2,1)} %fusion.7.refs_0_.refs_1_.refs_2_, bf16[1024,1536]{1,0:T(8,128)(2,1)} %fusion.7.refs_0_.refs_1_.refs_2_, bf16[1024,1536]{1,0:T(8,128)(2,1)} %fusion.7.refs_0_.refs_1_.refs_2_, ...), custom_call_target="tpu_custom_call" | custom-call | flops 1 | bytes 1024 | tf_op jit(solution)/shard_map/pallas_call | solution.py:218
  420.9 5.7 %fusion.5 = bf16[1024,1024]{0,1:T(8,128)(2,1)S(1)} fusion(bf16[1024,1536]{1,0:T(8,128)(2,1)S(1)} %constant_dynamic-update-slice_fusion.2, bf16[1024,2176]{1,0:T(8,128)(2,1)} %copy-done.26), kind=kOutput, calls=%fused_computation.34 | convolution fusion | flops 3221225472 | bytes 8388608 | tf_op jit(solution)/shard_map/dot_general | solution.py:23
  426.6 3.6 fusion.69
  450.8 4.7 fusion.18
  455.6 19.3 %collective-permute-done.26 = bf16[2,2,2,64,1024]{4,3,2,1,0:T(8,128)(2,1)} collective-permute-done((bf16[2,2,2,64,1024]{4,3,2,1,0:T(8,128)(2,1)}, bf16[2,2,2,64,1024]{4,3,2,1,0:T(8,128)(2,1)}, u32[]{:S(2)}, u32[]{:S(2)}) %collective-permute-start.26) | collective-permute-done | bytes 1048608 | tf_op jit(solution)/shard_map/ppermute | solution.py:247
  485.1 7.9 %collective-permute-done.37 = bf16[2,64,2048]{2,1,0:T(8,128)(2,1)S(1)} collective-permute-done((bf16[2,64,2048]{2,1,0:T(8,128)(2,1)S(1)}, bf16[2,64,2048]{2,1,0:T(8,128)(2,1)S(1)}, u32[]{:S(2)}, u32[]{:S(2)}) %collective-permute-start.37) | collective-permute-done | bytes 524320 | tf_op jit(solution)/shard_map/ppermute | solution.py:247
  493.3 5.9 %collective-permute-done.36 = f32[8,1024]{1,0:T(8,128)S(1)} collective-permute-done((f32[8,1024]{1,0:T(8,128)S(1)}, f32[8,1024]{1,0:T(8,128)S(1)}, u32[]{:S(2)}, u32[]{:S(2)}) %collective-permute-start.36) | collective-permute-done | bytes 32800 | tf_op jit(solution)/shard_map/ppermute | solution.py:247
  500.0 10.7 %collective-permute-done.38 = bf16[64,2048]{1,0:T(8,128)(2,1)S(1)} collective-permute-done((bf16[64,2048]{1,0:T(8,128)(2,1)S(1)}, bf16[64,2048]{1,0:T(8,128)(2,1)S(1)}, u32[]{:S(2)}, u32[]{:S(2)}) %collective-permute-start.38) | collective-permute-done | bytes 262176 | tf_op jit(solution)/shard_map/ppermute | solution.py:247
  523.3 16.2 %collective-permute-done.39 = bf16[2,64,2048]{2,1,0:T(8,128)(2,1)S(1)} collective-permute-done((bf16[2,64,2048]{2,1,0:T(8,128)(2,1)S(1)}, bf16[2,64,2048]{2,1,0:T(8,128)(2,1)S(1)}, u32[]{:S(2)}, u32[]{:S(2)}) %collective-permute-start.39) | collective-permute-done | bytes 524320 | tf_op jit(solution)/shard_map/ppermute | solution.py:247
  545.2 3.0 copy.104
  (347 shorter events, 163.8 us)
Async XLA Ops:
  7.2 58.4 %all-gather.5.cloned.1.call-start = ((), (), s32[]{:S(2)}) async-start(), calls=%async_computation.2 | async-start | bytes 4734976 | tf_op jit(solution)/shard_map/all_gather | solution.py:266
  10.6 106.8 %all-gather.7.cloned.1.call-start = ((), (), s32[]{:S(2)}) async-start(), calls=%async_computation.3 | async-start | bytes 4456448 | tf_op jit(solution)/shard_map/all_gather | solution.py:266
  12.4 160.8 %all-gather.9.cloned.1.call-start = ((), (), s32[]{:S(2)}) async-start(), calls=%async_computation.4 | async-start | bytes 4456448 | tf_op jit(solution)/shard_map/all_gather | solution.py:266
  18.0 18.6 %collective-permute-start.2 = (bf16[1024,1024]{0,1:T(8,128)(2,1)S(1)}, bf16[1024,1024]{0,1:T(8,128)(2,1)}, u32[]{:S(2)}, u32[]{:S(2)}) collective-permute-start(bf16[1024,1024]{0,1:T(8,128)(2,1)S(1)} %pad_maximum_fusion), channel_id=1, source_target_pairs={{1,2},{2,1},{5,6},{6,5},{9,10},{10,9},{13,14},{14,13},{17,18},{18,... | collective-permute-start | bytes 6291464 | tf_op jit(solution)/shard_map/ppermute | solution.py:247
  21.3 15.3 %collective-permute-start.1 = (bf16[512,1024]{0,1:T(8,128)(2,1)}, bf16[512,1024]{0,1:T(8,128)(2,1)}, u32[]{:S(2)}, u32[]{:S(2)}) collective-permute-start(bf16[512,1024]{0,1:T(8,128)(2,1)} %copy.83), channel_id=1, source_target_pairs={{1,2},{2,1},{5,6},{6,5},{9,10},{10,9},{13,14},{14,13},{17,18},{18,... | collective-permute-start | bytes 3145736 | tf_op jit(solution)/shard_map/ppermute | solution.py:247
  22.9 7.7 %collective-permute-start.3 = (bf16[64,2048]{1,0:T(8,128)(2,1)S(1)}, bf16[64,2048]{1,0:T(8,128)(2,1)}, u32[]{:S(2)}, u32[]{:S(2)}) collective-permute-start(bf16[64,2048]{1,0:T(8,128)(2,1)S(1)} %copy-done.49), channel_id=1, source_target_pairs={{1,2},{2,1},{5,6},{6,5},{9,10},{10,9},{13,14},{14,13},{17,18},{18,... | collective-permute-start | bytes 786440 | tf_op jit(solution)/shard_map/ppermute | solution.py:247
  24.3 12.3 %collective-permute-start.4 = (bf16[64,2048]{1,0:T(8,128)(2,1)S(1)}, bf16[64,2048]{1,0:T(8,128)(2,1)}, u32[]{:S(2)}, u32[]{:S(2)}) collective-permute-start(bf16[64,2048]{1,0:T(8,128)(2,1)S(1)} %copy-done.49), channel_id=1, source_target_pairs={{0,1},{1,3},{3,2},{2,0},{4,5},{5,7},{7,6},{6,4},{8,9},{9,11},{11,1... | collective-permute-start | bytes 786440 | tf_op jit(solution)/shard_map/ppermute | solution.py:247
  30.5 212.8 %all-gather.11.cloned.1.call-start = ((), (), s32[]{:S(2)}) async-start(), calls=%async_computation.5 | async-start | bytes 4718592 | tf_op jit(solution)/shard_map/all_gather | solution.py:278
  66.1 11.4 %collective-permute-start.9 = (s32[4,128]{1,0:T(4,128)S(1)}, s32[4,128]{1,0:T(4,128)S(1)}, u32[]{:S(2)}, u32[]{:S(2)}) collective-permute-start(s32[4,128]{1,0:T(4,128)S(1)} %slice.167), channel_id=1, source_target_pairs={{0,2},{1,3},{2,0},{3,1},{4,6},{5,7},{6,4},{7,5},{8,10},{9,11},{10,... | collective-permute-start | bytes 6152 | tf_op jit(solution)/shard_map/ppermute | solution.py:247
  69.0 8.8 %collective-permute-start.8 = (bf16[512,1024]{0,1:T(8,128)(2,1)}, bf16[512,1024]{0,1:T(8,128)(2,1)}, u32[]{:S(2)}, u32[]{:S(2)}) collective-permute-start(bf16[512,1024]{0,1:T(8,128)(2,1)} %slice.212), channel_id=1, source_target_pairs={{0,2},{1,3},{2,0},{3,1},{4,6},{5,7},{6,4},{7,5},{8,10},{9,11},{10,... | collective-permute-start | bytes 3145736 | tf_op jit(solution)/shard_map/ppermute | solution.py:247
  71.1 16.1 %collective-permute-start.5 = (bf16[1024,2176]{1,0:T(8,128)(2,1)}, bf16[1024,2176]{1,0:T(8,128)(2,1)}, u32[]{:S(2)}, u32[]{:S(2)}) collective-permute-start(bf16[1024,2176]{1,0:T(8,128)(2,1)} %all-gather.5.cloned.1.call-done), channel_id=1, source_target_pairs={{1,2},{2,1},{5,6},{6,5},{9,10},{10,9},{13,14},{14,13},{17,18},{18,... | collective-permute-start | bytes 13369352 | tf_op jit(solution)/shard_map/ppermute | solution.py:247
  75.1 6.5 %collective-permute-start.6 = (bf16[512,1024]{0,1:T(8,128)(2,1)S(1)}, bf16[512,1024]{0,1:T(8,128)(2,1)}, u32[]{:S(2)}, u32[]{:S(2)}) collective-permute-start(bf16[512,1024]{0,1:T(8,128)(2,1)S(1)} %broadcast_select_fusion.9), channel_id=1, source_target_pairs={{0,2},{1,3},{2,0},{3,1},{4,6},{5,7},{6,4},{7,5},{8,10},{9,11},{10,... | collective-permute-start | bytes 3145736 | tf_op jit(solution)/shard_map/ppermute | solution.py:247
  79.9 5.1 collective-permute-start.7
  117.4 59.1 %collective-permute-start.11 = (bf16[1024,2048]{1,0:T(8,128)(2,1)}, bf16[1024,2048]{1,0:T(8,128)(2,1)}, u32[]{:S(2)}, u32[]{:S(2)}) collective-permute-start(bf16[1024,2048]{1,0:T(8,128)(2,1)} %all-gather.7.cloned.1.call-done), channel_id=1, source_target_pairs={{1,2},{2,1},{5,6},{6,5},{9,10},{10,9},{13,14},{14,13},{17,18},{18,... | collective-permute-start | bytes 12582920 | tf_op jit(solution)/shard_map/ppermute | solution.py:247
  147.7 17.9 %collective-permute-start.10 = (bf16[1024,1024]{0,1:T(8,128)(2,1)}, bf16[1024,1024]{0,1:T(8,128)(2,1)}, u32[]{:S(2)}, u32[]{:S(2)}) collective-permute-start(bf16[1024,1024]{0,1:T(8,128)(2,1)} %fusion.45), channel_id=1, source_target_pairs={{0,2},{1,3},{2,0},{3,1},{4,6},{5,7},{6,4},{7,5},{8,10},{9,11},{10,... | collective-permute-start | bytes 6291464 | tf_op jit(solution)/shard_map/ppermute | solution.py:247
  163.3 389.3 %reduce-scatter.5.cloned.1.call-start = ((), (), s32[]{:S(2)}) async-start(), calls=%async_computation.7 | async-start | bytes 4456448 | tf_op jit(solution)/shard_map/reduce_scatter | solution.py:281
  173.2 46.7 %collective-permute-start.13 = (bf16[1024,2048]{1,0:T(8,128)(2,1)}, bf16[1024,2048]{1,0:T(8,128)(2,1)}, u32[]{:S(2)}, u32[]{:S(2)}) collective-permute-start(bf16[1024,2048]{1,0:T(8,128)(2,1)} %all-gather.9.cloned.1.call-done), channel_id=1, source_target_pairs={{1,2},{2,1},{5,6},{6,5},{9,10},{10,9},{13,14},{14,13},{17,18},{18,... | collective-permute-start | bytes 12582920 | tf_op jit(solution)/shard_map/ppermute | solution.py:247
  206.1 8.2 %collective-permute-start.12 = (bf16[1024,1024]{0,1:T(8,128)(2,1)}, bf16[1024,1024]{0,1:T(8,128)(2,1)}, u32[]{:S(2)}, u32[]{:S(2)}) collective-permute-start(bf16[1024,1024]{0,1:T(8,128)(2,1)} %fusion.38), channel_id=1, source_target_pairs={{0,2},{1,3},{2,0},{3,1},{4,6},{5,7},{6,4},{7,5},{8,10},{9,11},{10,... | collective-permute-start | bytes 6291464 | tf_op jit(solution)/shard_map/ppermute | solution.py:247
  256.0 23.1 %collective-permute-start.14 = (bf16[1024,1024]{0,1:T(8,128)(2,1)S(1)}, bf16[1024,1024]{0,1:T(8,128)(2,1)S(1)}, u32[]{:S(2)}, u32[]{:S(2)}) collective-permute-start(bf16[1024,1024]{0,1:T(8,128)(2,1)S(1)} %fusion.26), channel_id=1, source_target_pairs={{0,2},{1,3},{2,0},{3,1},{4,6},{5,7},{6,4},{7,5},{8,10},{9,11},{10,... | collective-permute-start | bytes 6291464 | tf_op jit(solution)/shard_map/ppermute | solution.py:247
  265.5 11.5 %collective-permute-start.33 = (bf16[512,1024]{0,1:T(8,128)(2,1)S(1)}, bf16[512,1024]{0,1:T(8,128)(2,1)S(1)}, u32[]{:S(2)}, u32[]{:S(2)}) collective-permute-start(bf16[512,1024]{0,1:T(8,128)(2,1)S(1)} %broadcast_select_fusion.10), channel_id=1, source_target_pairs={{0,2},{1,3},{2,0},{3,1},{4,6},{5,7},{6,4},{7,5},{8,10},{9,11},{10,... | collective-permute-start | bytes 3145736 | tf_op jit(solution)/shard_map/ppermute | solution.py:247
  265.7 56.1 %collective-permute-start.15 = (bf16[1024,2048]{1,0:T(8,128)(2,1)}, bf16[1024,2048]{1,0:T(8,128)(2,1)}, u32[]{:S(2)}, u32[]{:S(2)}) collective-permute-start(bf16[1024,2048]{1,0:T(8,128)(2,1)} %fusion.65), channel_id=1, source_target_pairs={{1,2},{2,1},{5,6},{6,5},{9,10},{10,9},{13,14},{14,13},{17,18},{18,... | collective-permute-start | bytes 12582920 | tf_op jit(solution)/shard_map/ppermute | solution.py:247
  274.5 96.9 %collective-permute-start.20 = (bf16[1024,2048]{1,0:T(8,128)(2,1)}, bf16[1024,2048]{1,0:T(8,128)(2,1)}, u32[]{:S(2)}, u32[]{:S(2)}) collective-permute-start(bf16[1024,2048]{1,0:T(8,128)(2,1)} %fusion.68), channel_id=1, source_target_pairs={{1,2},{2,1},{5,6},{6,5},{9,10},{10,9},{13,14},{14,13},{17,18},{18,... | collective-permute-start | bytes 12582920 | tf_op jit(solution)/shard_map/ppermute | solution.py:247
  328.5 26.4 %collective-permute-start.19 = (bf16[1024,1024]{0,1:T(8,128)(2,1)}, bf16[1024,1024]{0,1:T(8,128)(2,1)}, u32[]{:S(2)}, u32[]{:S(2)}) collective-permute-start(bf16[1024,1024]{0,1:T(8,128)(2,1)} %fusion.40), channel_id=1, source_target_pairs={{0,2},{1,3},{2,0},{3,1},{4,6},{5,7},{6,4},{7,5},{8,10},{9,11},{10,... | collective-permute-start | bytes 6291464 | tf_op jit(solution)/shard_map/ppermute | solution.py:247
  334.2 220.2 %reduce-scatter.3.cloned.1.call-start = ((), (), s32[]{:S(2)}) async-start(), calls=%async_computation.6 | async-start | bytes 4456448 | tf_op jit(solution)/shard_map/reduce_scatter | solution.py:281
  336.8 13.3 %collective-permute-start.34 = (bf16[512,1024]{0,1:T(8,128)(2,1)}, bf16[512,1024]{0,1:T(8,128)(2,1)}, u32[]{:S(2)}, u32[]{:S(2)}) collective-permute-start(bf16[512,1024]{0,1:T(8,128)(2,1)} %broadcast_select_fusion.11), channel_id=1, source_target_pairs={{0,2},{1,3},{2,0},{3,1},{4,6},{5,7},{6,4},{7,5},{8,10},{9,11},{10,... | collective-permute-start | bytes 3145736 | tf_op jit(solution)/shard_map/ppermute | solution.py:247
  349.3 35.4 %collective-permute-start.18 = (bf16[2,2,2,64,1024]{4,3,2,1,0:T(8,128)(2,1)S(1)}, bf16[2,2,2,64,1024]{4,3,2,1,0:T(8,128)(2,1)S(1)}, u32[]{:S(2)}, u32[]{:S(2)}) collective-permute-start(bf16[2,2,2,64,1024]{4,3,2,1,0:T(8,128)(2,1)S(1)} %get-tuple-element.263), channel_id=1, source_target_pairs={{0,4},{1,5},{2,6},{3,7},{4,0},{5,1},{6,2},{7,3},{8,12},{9,13},{10,... | collective-permute-start | bytes 3145736 | tf_op jit(solution)/shard_map/ppermute | solution.py:247
  350.1 34.6 %collective-permute-start.17 = (bf16[2,2,2,64,1024]{4,3,2,1,0:T(8,128)(2,1)S(1)}, bf16[2,2,2,64,1024]{4,3,2,1,0:T(8,128)(2,1)S(1)}, u32[]{:S(2)}, u32[]{:S(2)}) collective-permute-start(bf16[2,2,2,64,1024]{4,3,2,1,0:T(8,128)(2,1)S(1)} %get-tuple-element.265), channel_id=1, source_target_pairs={{1,0},{3,1},{2,3},{0,2},{5,4},{7,5},{6,7},{4,6},{9,8},{11,9},{10,1... | collective-permute-start | bytes 3145736 | tf_op jit(solution)/shard_map/ppermute | solution.py:247
  350.2 34.5 %collective-permute-start.16 = (bf16[2,2,2,64,1024]{4,3,2,1,0:T(8,128)(2,1)S(1)}, bf16[2,2,2,64,1024]{4,3,2,1,0:T(8,128)(2,1)S(1)}, u32[]{:S(2)}, u32[]{:S(2)}) collective-permute-start(bf16[2,2,2,64,1024]{4,3,2,1,0:T(8,128)(2,1)S(1)} %get-tuple-element.131), channel_id=1, source_target_pairs={{1,2},{2,1},{5,6},{6,5},{9,10},{10,9},{13,14},{14,13},{17,18},{18,... | collective-permute-start | bytes 3145736 | tf_op jit(solution)/shard_map/ppermute | solution.py:247
  354.9 144.3 %collective-permute-start.35 = (bf16[1024,1024]{0,1:T(8,128)(2,1)}, bf16[1024,1024]{0,1:T(8,128)(2,1)}, u32[]{:S(2)}, u32[]{:S(2)}) collective-permute-start(bf16[1024,1024]{0,1:T(8,128)(2,1)} %pad_maximum_fusion.6), channel_id=1, source_target_pairs={{1,2},{2,1},{5,6},{6,5},{9,10},{10,9},{13,14},{14,13},{17,18},{18,... | collective-permute-start | bytes 6291464 | tf_op jit(solution)/shard_map/ppermute | solution.py:247
  386.2 34.4 %collective-permute-start.21 = (bf16[2,2,64,1024]{3,2,1,0:T(8,128)(2,1)}, bf16[2,2,64,1024]{3,2,1,0:T(8,128)(2,1)}, u32[]{:S(2)}, u32[]{:S(2)}) collective-permute-start(bf16[2,2,64,1024]{3,2,1,0:T(8,128)(2,1)} %get-tuple-element.278), channel_id=1, source_target_pairs={{0,4},{1,5},{2,6},{3,7},{4,0},{5,1},{6,2},{7,3},{8,12},{9,13},{10,... | collective-permute-start | bytes 1572872 | tf_op jit(solution)/shard_map/ppermute | solution.py:247
  388.1 32.6 %collective-permute-start.23 = (bf16[2,2,64,1024]{3,2,1,0:T(8,128)(2,1)}, bf16[2,2,64,1024]{3,2,1,0:T(8,128)(2,1)}, u32[]{:S(2)}, u32[]{:S(2)}) collective-permute-start(bf16[2,2,64,1024]{3,2,1,0:T(8,128)(2,1)} %get-tuple-element.276), channel_id=1, source_target_pairs={{1,0},{3,1},{2,3},{0,2},{5,4},{7,5},{6,7},{4,6},{9,8},{11,9},{10,1... | collective-permute-start | bytes 1572872 | tf_op jit(solution)/shard_map/ppermute | solution.py:247
  388.1 32.6 %collective-permute-start.22 = (bf16[2,2,64,1024]{3,2,1,0:T(8,128)(2,1)S(1)}, bf16[2,2,64,1024]{3,2,1,0:T(8,128)(2,1)}, u32[]{:S(2)}, u32[]{:S(2)}) collective-permute-start(bf16[2,2,64,1024]{3,2,1,0:T(8,128)(2,1)S(1)} %get-tuple-element.153), channel_id=1, source_target_pairs={{1,2},{2,1},{5,6},{6,5},{9,10},{10,9},{13,14},{14,13},{17,18},{18,... | collective-permute-start | bytes 1572872 | tf_op jit(solution)/shard_map/ppermute | solution.py:247
  432.3 11.6 %collective-permute-start.27 = (bf16[512,1024]{0,1:T(8,128)(2,1)S(1)}, bf16[512,1024]{0,1:T(8,128)(2,1)S(1)}, u32[]{:S(2)}, u32[]{:S(2)}) collective-permute-start(bf16[512,1024]{0,1:T(8,128)(2,1)S(1)} %broadcast_select_fusion.12), channel_id=1, source_target_pairs={{0,2},{1,3},{2,0},{3,1},{4,6},{5,7},{6,4},{7,5},{8,10},{9,11},{10,... | collective-permute-start | bytes 3145736 | tf_op jit(solution)/shard_map/ppermute | solution.py:247
  435.1 20.5 %collective-permute-start.25 = (bf16[2,2,2,64,1024]{4,3,2,1,0:T(8,128)(2,1)}, bf16[2,2,2,64,1024]{4,3,2,1,0:T(8,128)(2,1)}, u32[]{:S(2)}, u32[]{:S(2)}) collective-permute-start(bf16[2,2,2,64,1024]{4,3,2,1,0:T(8,128)(2,1)} %get-tuple-element.261), channel_id=1, source_target_pairs={{1,0},{3,1},{2,3},{0,2},{5,4},{7,5},{6,7},{4,6},{9,8},{11,9},{10,1... | collective-permute-start | bytes 3145736 | tf_op jit(solution)/shard_map/ppermute | solution.py:247
  435.1 20.5 %collective-permute-start.24 = (bf16[2,2,2,64,1024]{4,3,2,1,0:T(8,128)(2,1)}, bf16[2,2,2,64,1024]{4,3,2,1,0:T(8,128)(2,1)}, u32[]{:S(2)}, u32[]{:S(2)}) collective-permute-start(bf16[2,2,2,64,1024]{4,3,2,1,0:T(8,128)(2,1)} %get-tuple-element.144), channel_id=1, source_target_pairs={{1,2},{2,1},{5,6},{6,5},{9,10},{10,9},{13,14},{14,13},{17,18},{18,... | collective-permute-start | bytes 3145736 | tf_op jit(solution)/shard_map/ppermute | solution.py:247
  439.0 36.0 %collective-permute-start.26 = (bf16[2,2,2,64,1024]{4,3,2,1,0:T(8,128)(2,1)}, bf16[2,2,2,64,1024]{4,3,2,1,0:T(8,128)(2,1)}, u32[]{:S(2)}, u32[]{:S(2)}) collective-permute-start(bf16[2,2,2,64,1024]{4,3,2,1,0:T(8,128)(2,1)} %get-tuple-element.259), channel_id=1, source_target_pairs={{0,4},{1,5},{2,6},{3,7},{4,0},{5,1},{6,2},{7,3},{8,12},{9,13},{10,... | collective-permute-start | bytes 3145736 | tf_op jit(solution)/shard_map/ppermute | solution.py:247
  449.5 6.0 %collective-permute-start.29 = (f32[8,1024]{1,0:T(8,128)S(1)}, f32[8,1024]{1,0:T(8,128)S(1)}, u32[]{:S(2)}, u32[]{:S(2)}) collective-permute-start(f32[8,1024]{1,0:T(8,128)S(1)} %add.274), channel_id=1, source_target_pairs={{0,8},{1,9},{2,10},{3,11},{4,12},{5,13},{6,14},{7,15},{8,0},{9,1},... | collective-permute-start | bytes 98312 | tf_op jit(solution)/shard_map/ppermute | solution.py:247
  455.5 37.5 %collective-permute-start.37 = (bf16[2,64,2048]{2,1,0:T(8,128)(2,1)S(1)}, bf16[2,64,2048]{2,1,0:T(8,128)(2,1)S(1)}, u32[]{:S(2)}, u32[]{:S(2)}) collective-permute-start(bf16[2,64,2048]{2,1,0:T(8,128)(2,1)S(1)} %copy-done.48), channel_id=1, source_target_pairs={{0,16},{1,17},{2,18},{3,19},{4,20},{5,21},{6,22},{7,23},{8,24},{9,... | collective-permute-start | bytes 1572872 | tf_op jit(solution)/shard_map/ppermute | solution.py:247
  478.0 32.6 %collective-permute-start.30 = (bf16[2,2,64,1024]{3,2,1,0:T(8,128)(2,1)}, bf16[2,2,64,1024]{3,2,1,0:T(8,128)(2,1)S(1)}, u32[]{:S(2)}, u32[]{:S(2)}) collective-permute-start(bf16[2,2,64,1024]{3,2,1,0:T(8,128)(2,1)} %get-tuple-element.274), channel_id=1, source_target_pairs={{0,4},{1,5},{2,6},{3,7},{4,0},{5,1},{6,2},{7,3},{8,12},{9,13},{10,... | collective-permute-start | bytes 1572872 | tf_op jit(solution)/shard_map/ppermute | solution.py:247
  482.3 28.4 %collective-permute-start.32 = (bf16[2,2,64,1024]{3,2,1,0:T(8,128)(2,1)}, bf16[2,2,64,1024]{3,2,1,0:T(8,128)(2,1)}, u32[]{:S(2)}, u32[]{:S(2)}) collective-permute-start(bf16[2,2,64,1024]{3,2,1,0:T(8,128)(2,1)} %get-tuple-element.272), channel_id=1, source_target_pairs={{1,0},{3,1},{2,3},{0,2},{5,4},{7,5},{6,7},{4,6},{9,8},{11,9},{10,1... | collective-permute-start | bytes 1572872 | tf_op jit(solution)/shard_map/ppermute | solution.py:247
  483.6 27.0 %collective-permute-start.31 = (bf16[2,2,64,1024]{3,2,1,0:T(8,128)(2,1)S(1)}, bf16[2,2,64,1024]{3,2,1,0:T(8,128)(2,1)}, u32[]{:S(2)}, u32[]{:S(2)}) collective-permute-start(bf16[2,2,64,1024]{3,2,1,0:T(8,128)(2,1)S(1)} %get-tuple-element.158), channel_id=1, source_target_pairs={{1,2},{2,1},{5,6},{6,5},{9,10},{10,9},{13,14},{14,13},{17,18},{18,... | collective-permute-start | bytes 1572872 | tf_op jit(solution)/shard_map/ppermute | solution.py:247
  493.1 6.1 %collective-permute-start.36 = (f32[8,1024]{1,0:T(8,128)S(1)}, f32[8,1024]{1,0:T(8,128)S(1)}, u32[]{:S(2)}, u32[]{:S(2)}) collective-permute-start(f32[8,1024]{1,0:T(8,128)S(1)} %add.275), channel_id=1, source_target_pairs={{0,16},{1,17},{2,18},{3,19},{4,20},{5,21},{6,22},{7,23},{8,24},{9,... | collective-permute-start | bytes 98312 | tf_op jit(solution)/shard_map/ppermute | solution.py:247
  499.2 11.4 %collective-permute-start.38 = (bf16[64,2048]{1,0:T(8,128)(2,1)S(1)}, bf16[64,2048]{1,0:T(8,128)(2,1)S(1)}, u32[]{:S(2)}, u32[]{:S(2)}) collective-permute-start(bf16[64,2048]{1,0:T(8,128)(2,1)S(1)} %get-tuple-element.290), channel_id=1, source_target_pairs={{0,8},{1,9},{2,10},{3,11},{4,12},{5,13},{6,14},{7,15},{8,0},{9,1},... | collective-permute-start | bytes 786440 | tf_op jit(solution)/shard_map/ppermute | solution.py:247
  499.2 40.3 %collective-permute-start.40 = (bf16[512,1024]{0,1:T(8,128)(2,1)}, bf16[512,1024]{0,1:T(8,128)(2,1)S(1)}, u32[]{:S(2)}, u32[]{:S(2)}) collective-permute-start(bf16[512,1024]{0,1:T(8,128)(2,1)} %fusion.18), channel_id=1, source_target_pairs={{1,2},{2,1},{5,6},{6,5},{9,10},{10,9},{13,14},{14,13},{17,18},{18,... | collective-permute-start | bytes 3145736 | tf_op jit(solution)/shard_map/ppermute | solution.py:247
  510.6 8.6 %collective-permute-start.41 = (f32[8,1024]{1,0:T(8,128)S(1)}, f32[8,1024]{1,0:T(8,128)S(1)}, u32[]{:S(2)}, u32[]{:S(2)}) collective-permute-start(f32[8,1024]{1,0:T(8,128)S(1)} %add.281), channel_id=1, source_target_pairs={{0,4},{1,5},{2,6},{3,7},{4,0},{5,1},{6,2},{7,3},{8,12},{9,13},{10,... | collective-permute-start | bytes 98312 | tf_op jit(solution)/shard_map/ppermute | solution.py:247
  514.0 25.5 %collective-permute-start.39 = (bf16[2,64,2048]{2,1,0:T(8,128)(2,1)S(1)}, bf16[2,64,2048]{2,1,0:T(8,128)(2,1)S(1)}, u32[]{:S(2)}, u32[]{:S(2)}) collective-permute-start(bf16[2,64,2048]{2,1,0:T(8,128)(2,1)S(1)} %get-tuple-element.270), channel_id=1, source_target_pairs={{0,16},{1,17},{2,18},{3,19},{4,20},{5,21},{6,22},{7,23},{8,24},{9,... | collective-permute-start | bytes 1572872 | tf_op jit(solution)/shard_map/ppermute | solution.py:247
  519.3 4.0 collective-permute-start.42
  540.5 10.3 %collective-permute-start.43 = (bf16[64,2048]{1,0:T(8,128)(2,1)S(1)}, bf16[64,2048]{1,0:T(8,128)(2,1)}, u32[]{:S(2)}, u32[]{:S(2)}) collective-permute-start(bf16[64,2048]{1,0:T(8,128)(2,1)S(1)} %dynamic-slice_bitcast_fusion.16), channel_id=1, source_target_pairs={{0,8},{1,9},{2,10},{3,11},{4,12},{5,13},{6,14},{7,15},{8,0},{9,1},... | collective-permute-start | bytes 786440 | tf_op jit(solution)/shard_map/ppermute | solution.py:247
  (63 other events, 475.5 us)
Sparse Core Ops, SparseCore 0:
  10.9 54.6 all-gather.4
  68.3 49.0 all-gather.6
  119.6 49.2 all-gather.8
  171.4 71.8 all-gather.10
  334.3 80.9 reduce-scatter.4
  419.5 91.5 reduce-scatter.2
where the time goes:
time: 571 us; the launch traced here: 563 us
  waiting for transfers between devices  143 us (25%)
  other arithmetic  104 us (18%)
  matrix products  95 us (17%)
  Pallas kernels  82.3 us (14%)
  starting transfers between devices  79.4 us (14%)
  local copies, waits for them, and re-layouts  44.5 us (8%)
  between operations  15.8 us (3%)
    dot_general x21, matrix products, dot(): lax.dot_general(former, latter, (dims, ((), ())), preferred_element_type=...  95 us
    ppermute x44, waiting for transfers between devices, send(): return lax.ppermute(values, AXES, pairs)  86.6 us
    ppermute x44, starting transfers between devices, send(): return lax.ppermute(values, AXES, pairs)  79.2 us
    all_gather x3, waiting for transfers between devices, gather(): return lax.all_gather(shard, 'dp', axis=0, tiled=True)  52.7 us
    pallas_call x2, Pallas kernels, attention_back(): pl.pallas_call(functools.partial(attention_back_kernel, tree, block), gri...  48.2 us
    pallas_call x2, Pallas kernels, attention(): pl.pallas_call(functools.partial(attention_kernel, tree, block), grid=(pa...  34.1 us
    unnamed x133, local copies, waits for them, and re-layouts  25.4 us
    select_n x8, other arithmetic, cross_end(): return jnp.where(self.home, *pending)  17.1 us
  transfers between devices with their start and end apart: 50, of which 14 were waited for; matrix products, arithmetic and copies ran while one was open for 38% of the time, Pallas kernels for 15%

commit v1 on v0

--- a/solution.py
+++ b/solution.py
@@ -231,6 +231,26 @@
     )(*operands)
 
 
+def pick(values, index, axis):
+    return lax.dynamic_index_in_dim(values, index, axis, keepdims=False)
+
+
+class Pending:
+    def __init__(self, finish, *received):
+        self.finish, self.received = finish, list(received)
+
+    def end(self):
+        return self.finish(*self.received)
+
+
+def wait(pendings, *values, computed=()):
+    marks = [lax.slice(v, (0,) * v.ndim, (1,) * (v.ndim - 2) + (8, PAIR)) for v in computed]
+    received, values, _ = lax.optimization_barrier(([p.received for p in pendings], values, marks))
+    for pending, got in zip(pendings, received):
+        pending.received = got
+    return values
+
+
 class Links:
     def __init__(self, dp_size):
         self.devices = 2 * dp_size
@@ -246,114 +266,114 @@
     def send(self, values, pairs):
         return lax.ppermute(values, AXES, pairs)
 
+    def flip(self, values, bit):
+        return self.send(values, [(i, i ^ bit) for i in range(self.devices)])
+
     def quad(self, values, edges):
         pairs = [(4 * m + s, 4 * m + t) for m in range(self.places) for s, t in edges]
         return self.send(values, pairs)
 
-    def cross_begin(self, values):
-        return values, self.quad(values, [(1, 2), (2, 1)])
-
-    def cross_end(self, pending):
-        return jnp.where(self.home, *pending)
-
     def cross(self, values):
-        return self.cross_end(self.cross_begin(values))
+        return Pending(
+            lambda got: jnp.where(self.home, values, got), self.quad(values, [(1, 2), (2, 1)])
+        )
 
     def swap_cores(self, values):
         return self.quad(values, [(0, 2), (1, 3), (2, 0), (3, 1)])
 
+    def groups(self):
+        return [[2 * m + c for m in range(self.places)] for c in range(2)]
+
     def gather(self, shard):
         return lax.all_gather(shard, "dp", axis=0, tiled=True)
 
-    def sides_begin(self, shard):
-        return self.cross_begin(shard), self.quad(shard, [(0, 1), (1, 3), (3, 2), (2, 0)])
-
-    def gather_sides_first(self, pending):
-        former, latter = self.cross_end(pending[0]), pending[1]
-        first_side = self.side == 0
-        both = jnp.concatenate(
-            [jnp.where(first_side, former, latter), jnp.where(first_side, latter, former)], 0
-        )
-        groups = [[2 * m + c for m in range(self.places)] for c in range(2)]
-        return lax.all_gather(both, "dp", axis=0, tiled=True, axis_index_groups=groups)
-
-    def scatter(self, crossed):
-        return lax.psum_scatter(crossed, "dp", scatter_dimension=0, tiled=True).astype(F32)
+    def sides(self, shard):
+        def finish(near, far):
+            near = jnp.where(self.home, shard, near)
+            first = self.side == 0
+            return jnp.concatenate([jnp.where(first, near, far), jnp.where(first, far, near)], 0)
+
+        return Pending(
+            finish,
+            self.quad(shard, [(1, 2), (2, 1)]),
+            self.quad(shard, [(0, 1), (1, 3), (3, 2), (2, 0)]),
+        )
+
+    def gather_places(self, both):
+        return lax.all_gather(both, "dp", axis=0, tiled=True, axis_index_groups=self.groups())
+
+    def scatter(self, grad):
+        return lax.psum_scatter(grad, "dp", scatter_dimension=0, tiled=True)
+
+    def scatter_places(self, grad):
+        return lax.psum_scatter(
+            grad, "dp", scatter_dimension=0, tiled=True, axis_index_groups=self.groups()
+        )
+
+    def sides_back(self, parts, axis):
+        mine, other = (
+            jnp.concatenate([pick(part, index, axis) for part in parts], -1)
+            for index in (self.side, 1 - self.side)
+        )
+        return Pending(
+            lambda near, far: jnp.where(self.home, mine, near).astype(F32) + far.astype(F32),
+            self.quad(mine, [(1, 2), (2, 1)]),
+            self.quad(other, [(1, 0), (3, 1), (2, 3), (0, 2)]),
+        )
+
+    def halve(self, parts, axis, bit, index):
+        kept, sent = (
+            jnp.concatenate([pick(part, i, axis) for part in parts], -1) for i in (index, 1 - index)
+        )
+        return Pending(
+            lambda got: kept.astype(F32) + got.astype(F32), self.flip(sent, bit)
+        )
 
     def total(self, values, bits):
         if not self.grid:
             return lax.psum(values, AXES) if 1 in bits else values
         for bit in bits:
-            values = values + self.send(values, [(i, i ^ bit) for i in range(self.devices)])
+            values = values + self.flip(values, bit)
         return values
-
-
-def pick(values, index, axis):
-    return lax.dynamic_index_in_dim(values, index, axis, keepdims=False)
-
-
-def rounded_sum(former, latter):
-    return (former.astype(F32) + latter.astype(F32)).astype(BF)
-
-
-def together(*values):
-    return lax.optimization_barrier(values)
 
 
 class Scatter:
     def __init__(self, links, first, second):
         self.links = links
-        self.state = first, second
-
-    def exchange(self, values, axis, bit, index):
-        kept, sent = pick(values, index, axis), pick(values, 1 - index, axis)
-        return kept, self.links.send(sent, [(i, i ^ bit) for i in range(self.links.devices)])
-
-    def sides(self, values, axis):
-        links = self.links
-        former, latter = pick(values, links.side, axis), pick(values, 1 - links.side, axis)
-        return links.cross_begin(former), links.quad(latter, [(1, 0), (3, 1), (2, 3), (0, 2)])
-
-    def sides_end(self, pending):
-        return rounded_sum(self.links.cross_end(pending[0]), pending[1])
-
-    def first(self):
-        links = self.links
         if not links.grid:
-            whole = jnp.concatenate(self.state, 1)
-            self.state = links.scatter(links.cross(whole))
+            whole = links.scatter_places(jnp.concatenate(list(first) + list(second), 1))
+            self.state = [links.sides_back([whole.reshape(2, -1, whole.shape[1])], 0)]
             return
         former, latter = (
-            part.reshape(2, 2, 2, 2, part.shape[0] // 16, part.shape[1]) for part in self.state
-        )
-        self.state = self.sides(former, 3), self.exchange(latter, 2, 4, links.place % 2)
+            [part.reshape(2, 2, 2, 2, part.shape[0] // 16, part.shape[1]) for part in parts]
+            for parts in (first, second)
+        )
+        self.state = [
+            links.sides_back(former, 3), links.halve(latter, 2, 4, links.place % 2)
+        ]
 
     def second(self):
         links = self.links
         if links.grid:
-            former, latter = self.sides_end(self.state[0]), rounded_sum(*self.state[1])
-            self.state = self.exchange(former, 2, 4, links.place % 2), self.sides(latter, 2)
+            former, latter = (pending.end().astype(BF) for pending in self.state)
+            self.state = [
+                links.halve([former], 2, 4, links.place % 2), links.sides_back([latter], 2)
+            ]
 
     def far(self):
-        if self.links.grid:
-            both = jnp.concatenate(
-                [rounded_sum(*self.state[0]), self.sides_end(self.state[1])], -1
-            )
-            self.state = self.exchange(both, 0, 16, self.links.place // 4)
+        links = self.links
+        if links.grid:
+            both = jnp.concatenate([pending.end().astype(BF) for pending in self.state], -1)
+            self.state = [links.halve([both], 0, 16, links.place // 4)]
 
     def near(self):
-        if self.links.grid:
-            whole = rounded_sum(*self.state)
-            self.state = self.exchange(whole, 0, 8, self.links.place // 2 % 2)
+        links = self.links
+        if links.grid:
+            whole = self.state[0].end().astype(BF)
+            self.state = [links.halve([whole], 0, 8, links.place // 2 % 2)]
 
     def result(self):
-        if self.links.grid:
-            self.state = self.state[0].astype(F32) + self.state[1].astype(F32)
-        return self.state
-
-    def after(self, *values):
-        self.state, values = lax.optimization_barrier((self.state, values))
-        return values
+        return self.state[0].end()
 
 
 def ancestor_bits(segment_all, parent_row):
@@ -429,17 +449,18 @@
             [jnp.where(first_core, mine, other), jnp.where(first_core, other, mine)], 0
         )
 
-    def my_half(values):
-        return jnp.where(first_core, values[:half], values[half:])
-
-    def other_half(values):
-        return jnp.where(first_core, values[half:], values[:half])
+    def my_half(values, first=first_core):
+        return jnp.where(first, values[:half], values[half:])
+
+    def other_half(values, first=first_core):
+        return jnp.where(first, values[half:], values[:half])
 
     def joined(part):
         return part.astype(F32) + links.swap_cores(part).astype(F32)
 
-    def joined_half(part):
-        return my_half(part).astype(F32) + links.swap_cores(other_half(part)).astype(F32)
+    def joined_half(part, first=first_core):
+        sent = links.swap_cores(other_half(part, first))
+        return my_half(part, first).astype(F32) + sent.astype(F32)
 
     nodes = parent.shape[1]
     labels = jnp.concatenate(
@@ -458,14 +479,13 @@
         jnp.concatenate([cross_query, cross_key, cross_value, cross_output], 1)
     )
     up_w = links.gather(ffn_up)
-    moved = links.cross_begin(labels), links.cross_begin(x_in)
-    others = links.cross_begin(jnp.concatenate([source, cotangent], 0))
-    down_w = links.sides_begin(ffn_down)
-    self_w, moved, others, down_w = together(self_w, moved, others, down_w)
-    down_w = links.gather_sides_first(down_w)
-    self_w = links.cross_begin(self_w)
-    labels, x_mine = links.cross_end(moved[0]), links.cross_end(moved[1])
-    others = links.cross_end(others)
+    moved = [links.cross(x_in), links.cross(labels), links.cross(jnp.concatenate([source, cotangent], 0))]
+    down_w = links.sides(ffn_down)
+    whole = Pending(lambda got: got, self_w)
+    wait(moved + [down_w, whole])
+    self_w = links.cross(whole.end())
+    down_w = links.gather_places(down_w.end())
+    x_mine, labels, others = (pending.end() for pending in moved)
     x_zero = both_halves(x_mine).astype(F32)
     segment_all = both_halves(labels[:segment_rows]).reshape(tokens)
     query_bits, key_bits = ancestor_bits(segment_all, labels[segment_rows, :nodes])
@@ -475,31 +495,32 @@
     grad_top = both_halves(others[half:])
     centered, inverse = norm_stats(x_zero)
     normed = centered * inverse
-    self_w, normed, source_all, grad_top = together(self_w, normed, source_all, grad_top)
-    self_w = links.cross_end(self_w)
+    whole = Pending(lambda got: got, cross_w)
+    wait([self_w, whole], computed=(normed, source_all, grad_top))
+    cross_w = links.cross(whole.end())
+    self_w = self_w.end()
     norms = self_w[:, four : four + 8].astype(F32).T
     gain = [norms[i : i + 1] for i in range(3)]
     shift = [norms[i + 3 : i + 4] for i in range(3)]
 
     hidden_one = (normed * gain[0] + shift[0]).astype(BF)
-    hidden_one, cross_w = together(hidden_one, cross_w)
-    cross_w = links.cross_begin(cross_w)
     qkv = mm(hidden_one, self_w[:, :three], BF)
     self_places = (0, pairs, 2 * pairs)
     mixed_one, lse_one = attention(qkv, qkv, qkv, self_places, pairs, forward_bits)
     x_one = x_zero + joined(mm_rt(mixed_one, self_w[:, three:four], BF))
     hidden_two = norm(x_one, gain[1], shift[1]).astype(BF)
-    hidden_two, up_w = together(hidden_two, up_w)
-    up_w = links.cross_begin(up_w)
-    cross_w = links.cross_end(cross_w)
+    whole = Pending(lambda got: got, up_w)
+    (hidden_two,) = wait([whole], hidden_two)
+    up_w = links.cross(whole.end())
+    cross_w = cross_w.end()
     cross_queries = mm(hidden_two, cross_w[:, :heads_width], BF)
     memory = mm(source_all, cross_w[:, heads_width:three], BF)
     cross_places = (0, 0, pairs)
     mixed_two, lse_two = attention(cross_queries, memory, memory, cross_places, pairs, None)
     x_two = x_one + joined(mm_rt(mixed_two, cross_w[:, three:four], BF))
     hidden_three = norm(x_two, gain[2], shift[2]).astype(BF)
-    hidden_three, up_w = together(hidden_three, up_w)
-    up_w = links.cross_end(up_w)
+    (hidden_three,) = wait([up_w], hidden_three)
+    up_w = up_w.end()
     active = mm(hidden_three, up_w)
     normal = 0.5 * (1.0 + lax.erf(active * np.float32(0.5**0.5)))
     slope = (
@@ -507,15 +528,16 @@
     ).astype(BF)
     activated = (active * normal).astype(BF)
     down_grad = mm_lt(grad_top, activated, BF)
-    down_w, down_grad, activated, slope = together(down_w, down_grad, activated, slope)
+    whole = Pending(lambda got: got, down_w)
+    down_grad, activated, slope = wait([whole], down_grad, activated, slope)
+    down_w = whole.end()
 
     def norm_sums(values, grad):
         return jnp.sum(my_half(values), 0), jnp.sum(my_half(grad), 0)
 
-    down_grad = links.cross_begin(down_grad)
+    down_grad = links.scatter_places(down_grad)
     active_grad = (mm(grad_top, down_w) * slope.astype(F32)).astype(BF)
-    up_grad = links.cross_begin(mm_lt(hidden_three, active_grad, BF))
-    out_part = mm_rt(activated, down_w, BF)
+    up_grad = links.cross(mm_lt(hidden_three, active_grad, BF))
     normed_grad = joined(mm_rt(active_grad, up_w, BF))
     back, gain_part = norm_back(x_two, gain[2], normed_grad)
     gain_three, shift_three = norm_sums(gain_part, normed_grad)
@@ -525,69 +547,72 @@
     dq, dk, dv = attention_back(
         cross_queries, memory, memory, mixed_two, lse_two, mixed_grad, cross_places, pairs, None
     )
-    dq, dk, dv, down_grad = together(dq, dk, dv, down_grad)
-    down_grad = links.scatter(links.cross_end(down_grad))
+    down_grad = Pending(lambda got: got, down_grad)
     part = mm_rt(dq, cross_w[:, :heads_width], BF)
+    dkv = jnp.concatenate([dk, dv], 1)
+    cross_q_grad = mm_lt(hidden_two, dq, BF)
+    cross_o_grad = mm_lt(grad_two_low, mixed_two, BF)
+    cross_kv_grad = mm_lt(source_all, dkv, BF)
     normed_grad = joined(part)
-    dkv = jnp.concatenate([dk, dv], 1)
-    cross_grad = Scatter(
-        links,
-        jnp.concatenate([mm_lt(hidden_two, dq, BF), mm_lt(grad_two_low, mixed_two, BF)], 1),
-        mm_lt(source_all, dkv, BF),
-    )
-    cross_grad.first()
-    back, gain_part = norm_back(x_one, gain[1], normed_grad)
+    (gain_row,) = wait([up_grad, down_grad], gain[1], computed=(part, cross_q_grad, cross_o_grad))
+    up_grad, gain_row = wait([], up_grad.end(), gain_row)
+    up_grad = Pending(lambda got: got, links.scatter(up_grad))
+    back, gain_part = norm_back(x_one, gain_row, normed_grad)
     gain_two, shift_two = norm_sums(gain_part, normed_grad)
     grad_one = grad_two + back
     grad_one_low = grad_one.astype(BF)
+    self_o_grad = mm_lt(grad_one_low, mixed_one, BF)
+    cross_grad = Scatter(
+        links,
+        [cross_q_grad, cross_o_grad, self_o_grad[:, : heads_width // 2]],
+        [cross_kv_grad, self_o_grad[:, heads_width // 2 :]],
+    )
     mixed_grad = mm(grad_one_low, self_w[:, three:four], BF)
-    mixed_grad, up_grad = cross_grad.after(mixed_grad, up_grad)
-    cross_grad.second()
-    up_grad = links.scatter(links.cross_end(up_grad))
-    x_three = (my_half(x_two) + joined_half(out_part)).astype(BF)
-    source_part = joined_half(mm_rt(dkv, cross_w[:, heads_width:three], BF)).astype(BF)
-    outs = links.cross_begin(jnp.concatenate([x_three, source_part], 0))
     dq, dk, dv = attention_back(
         qkv, qkv, qkv, mixed_one, lse_one, mixed_grad, self_places, pairs, backward_bits
     )
-    dq, dk, dv = cross_grad.after(dq, dk, dv)
-    cross_grad.far()
     dqkv = jnp.concatenate([dq, dk, dv], 1)
     qkv_grad = mm_lt(hidden_one, dqkv, BF)
-    self_grad = Scatter(
-        links,
-        qkv_grad[:, :two],
-        jnp.concatenate([qkv_grad[:, two:], mm_lt(grad_one_low, mixed_one, BF)], 1),
-    )
-    self_grad.first()
-    normed_grad = joined_half(mm_rt(dqkv, self_w[:, :three], BF))
-    back, gain_part = norm_back(my_half(x_zero), gain[0], normed_grad)
+    self_grad = links.cross(qkv_grad)
+    part = mm_rt(dqkv, self_w[:, :three], BF)
+    part, down_late, cross_late = wait(
+        cross_grad.state, part, down_w, cross_w, computed=(qkv_grad,)
+    )
+    cross_grad.second()
+    normed_grad = joined_half(part)
+    out_part = mm_rt(activated, down_late, BF)
+    source_part = mm_rt(dkv, cross_late[:, heads_width:three], BF)
+    wait([self_grad], computed=(out_part, source_part))
+    self_grad, first_late, gain_zero = wait([], self_grad.end(), first_core, gain[0])
+    self_grad = links.scatter(self_grad)
+    x_three = (my_half(x_two, first_late) + joined_half(out_part, first_late)).astype(BF)
+    source_part = joined_half(source_part, first_late).astype(BF)
+    outs = [links.cross(v) for v in (x_three, source_part)]
+    (gain_zero,) = wait(cross_grad.state, gain_zero)
+    cross_grad.far()
+    back, gain_part = norm_back(my_half(x_zero), gain_zero, normed_grad)
     gain_one, shift_one = jnp.sum(gain_part, 0), jnp.sum(normed_grad, 0)
     x_grad_mine = (my_half(grad_one) + back).astype(BF)
     sums = jnp.stack(
         [gain_one, gain_two, gain_three, shift_one, shift_two, shift_three,
          jnp.zeros_like(gain_one), jnp.zeros_like(gain_one)]
     )
-    sums = links.total(sums, (2, 8))
-    x_grad_mine, sums = self_grad.after(x_grad_mine, sums)
-    self_grad.second()
+    (sums,) = wait(outs, sums, computed=(x_grad_mine,))
+    outs.append(links.cross(x_grad_mine))
+    down_grad = links.sides_back([down_grad.end().reshape(2, -1, hidden)], 0)
+    x_out, source_grad = (pending.end() for pending in outs[:2])
+    source_grad = source_grad.astype(F32)
+    up_grad = up_grad.end().astype(F32)
+    sums = links.total(sums, (2, 4))
+    (sums,) = wait(cross_grad.state + [down_grad], sums, computed=(source_grad, up_grad))
     cross_grad.near()
-    sums = links.total(sums, (16,))
-    outs, sums, cross_grad.state = self_grad.after(outs, sums, cross_grad.state)
-    self_grad.far()
+    down_grad = down_grad.end()
+    sums = links.total(sums, (8, 16, 1))
+    (sums,) = wait(cross_grad.state + outs[2:], sums, computed=(down_grad,))
+    x_grad = outs[2].end().astype(F32)
     cross_grad = cross_grad.result()
-    x_grad = links.cross_begin(x_grad_mine)
-    sums = links.total(sums, (4, 1))
-    outs = links.cross_end(outs)
-    x_out = outs[:half]
-    source_grad = outs[half:].astype(F32)
-    x_grad, sums, cross_grad, x_out, source_grad = self_grad.after(
-        x_grad, sums, cross_grad, x_out, source_grad
-    )
-    self_grad.near()
-    x_grad = links.cross_end(x_grad).astype(F32)
     norm_mine = lax.dynamic_slice(sums, (0, lax.axis_index("dp") * rows), (8, rows)).T
-    self_grad = self_grad.result()
+    self_grad = self_grad.astype(F32)
 
     def piece(values, number):
         return values[:, number * heads_width : (number + 1) * heads_width]
@@ -601,10 +626,12 @@
         piece(self_grad, 0),
         piece(self_grad, 1),
         piece(self_grad, 2),
-        piece(self_grad, 3),
+        jnp.concatenate(
+            [cross_grad[:, two : two + heads_width // 2], cross_grad[:, -(heads_width // 2) :]], 1
+        ),
         piece(cross_grad, 0),
-        piece(cross_grad, 2),
-        piece(cross_grad, 3),
+        cross_grad[:, two + heads_width // 2 : two + 3 * heads_width // 2],
+        cross_grad[:, two + 3 * heads_width // 2 : two + 5 * heads_width // 2],
         piece(cross_grad, 1),
         up_grad,
         down_grad,

time: 571 us -> 542 us (0.949)
  waiting for transfers between devices: 143 us -> 112 us
  starting transfers between devices: 79.4 us -> 88.6 us
  other arithmetic: 104 us -> 97.4 us
    ppermute x44 -> x39, waiting for transfers between devices: 86.6 us -> 20.9 us  [send(): return lax.ppermute(values, AXES, pairs)]
    reduce_scatter x2 -> x3, waiting for transfers between devices: 0.01 us -> 14.8 us  [the longest x2 7.68 us: scatter(): return lax.psum_scatter(grad, 'dp', scatter_dimension=0, tiled=True)]
    all_gather x3, waiting for transfers between devices: 52.7 us -> 66.3 us  [gather(): return lax.all_gather(shard, 'dp', axis=0, tiled=True)]
    ppermute x44 -> x39, starting transfers between devices: 79.2 us -> 88.1 us  [send(): return lax.ppermute(values, AXES, pairs)]
    all_gather x1, waiting for transfers between devices: 3.41 us -> 10.1 us  [gather_places(): lax.all_gather(both, 'dp', axis=0, tiled=True, axis_index_groups=self.gro...]
    convert_element_type x17 -> x10, other arithmetic: 21.7 us -> 15.1 us  [the longest x2 3.43 us: far(): pending.end().astype(BF)]
    concatenate x7 -> x6, other arithmetic: 9.38 us -> 3.44 us  [the longest x1 1.64 us: shards(): jnp.concatenate([source, cotangent], 0)]
    select_n x12 -> x11, other arithmetic: 20.9 us -> 18.9 us  [the longest x7 15.9 us: cross(): jnp.where(self.home, values, got)]
  transfers between devices with their start and end apart: 50 -> 46, of which waited for: 14 -> 14; matrix products, arithmetic and copies ran while one was open for 38% -> 37% of each run, Pallas kernels for 15% -> 15%
where the time goes in v1:
time: 542 us; the launch traced here: 536 us
  waiting for transfers between devices  112 us (21%)
  other arithmetic  97.4 us (18%)
  matrix products  92 us (17%)
  starting transfers between devices  88.6 us (16%)
  Pallas kernels  82.5 us (15%)
  local copies, waits for them, and re-layouts  47.2 us (9%)
  between operations  15.6 us (3%)
    dot_general x21, matrix products, dot(): lax.dot_general(former, latter, (dims, ((), ())), preferred_element_type=...  92 us
    ppermute x39, starting transfers between devices, send(): return lax.ppermute(values, AXES, pairs)  88.1 us
    all_gather x3, waiting for transfers between devices, gather(): return lax.all_gather(shard, 'dp', axis=0, tiled=True)  66.3 us
    pallas_call x2, Pallas kernels, attention_back(): pl.pallas_call(functools.partial(attention_back_kernel, tree, block), gri...  48.4 us
    pallas_call x2, Pallas kernels, attention(): pl.pallas_call(functools.partial(attention_kernel, tree, block), grid=(pa...  34.1 us
    unnamed x173, local copies, waits for them, and re-layouts  25.8 us
    ppermute x39, waiting for transfers between devices, send(): return lax.ppermute(values, AXES, pairs)  20.9 us
    select_n x7, other arithmetic, cross(): jnp.where(self.home, values, got)  15.9 us
  transfers between devices with their start and end apart: 46, of which 14 were waited for; matrix products, arithmetic and copies ran while one was open for 37% of the time, Pallas kernels for 15%

profile of v1, /device:TPU:0, one launch (start us, length us, event | category | flops | bytes accessed | tf_op | source)
XLA Modules:
  0.0 535.6 jit_solution(535463254102400902)
XLA Ops:
  21.1 7.1 %collective-permute-start.4 = (bf16[64,2048]{1,0:T(8,128)(2,1)S(1)}, bf16[64,2048]{1,0:T(8,128)(2,1)S(1)}, u32[]{:S(2)}, u32[]{:S(2)}) collective-permute-start(bf16[64,2048]{1,0:T(8,128)(2,1)S(1)} %copy-done.59), channel_id=1, source_target_pairs={{0,1},{1,3},{3,2},{2,0},{4,5},{5,7},{7,6},{6,4},{8,9},{9,11},{11,1... | collective-permute-start | bytes 786440 | tf_op jit(solution)/shard_map/ppermute | solution.py:267
  29.0 6.0 %collective-permute-done.4 = bf16[64,2048]{1,0:T(8,128)(2,1)S(1)} collective-permute-done((bf16[64,2048]{1,0:T(8,128)(2,1)S(1)}, bf16[64,2048]{1,0:T(8,128)(2,1)S(1)}, u32[]{:S(2)}, u32[]{:S(2)}) %collective-permute-start.4) | collective-permute-done | bytes 262176 | tf_op jit(solution)/shard_map/ppermute | solution.py:267
  36.6 28.9 %all-gather.5.cloned.1.call-done = bf16[1024,2176]{1,0:T(8,128)(2,1)} async-done(((bf16[64,2176]{1,0:T(8,128)(2,1)}), bf16[1024,2176]{1,0:T(8,128)(2,1)}) %all-gather.5.cloned.1.call-update) | async-done | bytes 4456464 | tf_op jit(solution)/shard_map/all_gather | solution.py:288
  65.6 2.8 collective-permute-start.6
  81.7 35.9 %all-gather.7.cloned.1.call-done = bf16[1024,2048]{1,0:T(8,128)(2,1)} async-done(((bf16[64,2048]{1,0:T(8,128)(2,1)}), bf16[1024,2048]{1,0:T(8,128)(2,1)}) %all-gather.7.cloned.1.call-update) | async-done | bytes 4194320 | tf_op jit(solution)/shard_map/all_gather | solution.py:288
  125.6 5.4 %fusion.7.refs_0_.refs_1_.refs_2_ = bf16[1024,1536]{1,0:T(8,128)(2,1)} fusion(bf16[1024,2176]{1,0:T(8,128)(2,1)S(1)} %broadcast_select_fusion, f32[1024]{0:T(1024)S(1)} %get-tuple-element.230, f32[1024]{0:T(1024)S(1)} %get-tuple-element.234, f32[1024]{0:T(1024)S(1)} %add_rsqrt_fusion.2, f32[1024]{0:T(1024)S(1)} %broadcast_multiply_fusion.6, ...), kind=kOutput, calls=%fused_computation.35 | convolution fusion | flops 3230662656 | bytes 8404992 | tf_op jit(solution)/shard_map/dot_general | solution.py:23
  131.0 15.0 %shard_map.280 = (bf16[1024,512]{1,0:T(8,128)(2,1)S(1)}, f32[1024,512]{1,0:T(8,128)S(1)}) custom-call(bf16[1024,1536]{1,0:T(8,128)(2,1)} %fusion.7.refs_0_.refs_1_.refs_2_, bf16[1024,1536]{1,0:T(8,128)(2,1)} %fusion.7.refs_0_.refs_1_.refs_2_, bf16[1024,1536]{1,0:T(8,128)(2,1)} %fusion.7.refs_0_.refs_1_.refs_2_, s32[1024,1]{1,0:T(8,128)S(1)} %copy.94.refs_3_, ...), custom_call_target="tpu_custom_call" | custom-call | flops 1 | bytes 1024 | tf_op jit(solution)/shard_map/pallas_call | solution.py:117
  150.5 3.1 broadcast_select_fusion.15
  156.8 3.0 broadcast_select_fusion.13
  159.8 3.5 fusion.65
  168.9 2.9 collective-permute-start.13
  174.4 3.7 fusion.19.refs_1_.refs_2_
  179.4 19.1 %shard_map.281 = (bf16[1024,512]{1,0:T(8,128)(2,1)S(1)}, f32[1024,512]{1,0:T(8,128)}) custom-call(bf16[1024,512]{1,0:T(8,128)(2,1)S(1)} %fusion.44.refs_0_, bf16[1024,1024]{1,0:T(8,128)(2,1)} %fusion.19.refs_1_.refs_2_, bf16[1024,1024]{1,0:T(8,128)(2,1)} %fusion.19.refs_1_.refs_2_), custom_call_target="tpu_custom_call" | custom-call | flops 1 | bytes 1024 | tf_op jit(solution)/shard_map/pallas_call | solution.py:117
  202.2 3.9 collective-permute-done.12
  206.1 4.6 fusion.64
  215.2 9.3 %fusion.4 = (bf16[1024,2048]{1,0:T(8,128)(2,1)}, bf16[1024,2048]{1,0:T(8,128)(2,1)S(1)}) fusion(bf16[1024,1024]{0,1:T(8,128)(2,1)S(1)} %add_convert_fusion, bf16[1024,2048]{1,0:T(8,128)(2,1)S(1)} %copy-done.75, bf16[1024,2048]{1,0:T(8,128)(2,1)} %collective-permute-done.13, pred[]{:T(512)S(6)} %eq.91), kind=kOutput, calls=%fused_computation.5 | convolution fusion | flops 4320133120 | bytes 18874368 | tf_op jit(solution)/shard_map/dot_general | solution.py:23
  226.5 6.1 %fusion.53 = bf16[1024,2048]{1,0:T(8,128)(2,1)} fusion(bf16[1024,2048]{1,0:T(8,128)(2,1)S(1)} %get-tuple-element.96, bf16[512,1024]{0,1:T(8,128)(2,1)S(1)} %copy-done.37, bf16[512,1024]{0,1:T(8,128)(2,1)S(1)} %copy-done.35), kind=kOutput, calls=%fused_computation.131 | convolution fusion | flops 4299161600 | bytes 10485760 | tf_op jit(solution)/shard_map/dot_general | solution.py:23
  232.7 10.1 %all-gather.11.cloned.1.call-done = bf16[1024,2048]{1,0:T(8,128)(2,1)} async-done(((bf16[128,2048]{1,0:T(8,128)(2,1)}), bf16[1024,2048]{1,0:T(8,128)(2,1)}) %all-gather.11.cloned.1.call-update) | async-done | bytes 4194320 | tf_op jit(solution)/shard_map/all_gather | solution.py:303
  242.9 8.7 %multiply_convert_fusion = bf16[1024,2048]{1,0:T(8,128)(2,1)S(1)} fusion(bf16[1024,2048]{1,0:T(8,128)(2,1)} %get-tuple-element.85, bf16[1024,2048]{1,0:T(8,128)(2,1)} %all-gather.11.cloned.1.call-done, bf16[512,1024]{0,1:T(8,128)(2,1)} %get-tuple-element.198, bf16[512,1024]{0,1:T(8,128)(2,1)} %get-tuple-element.197), kind=kOutput, calls=%fused_computation.6 | convolution fusion | flops 4305453056 | bytes 14680064 | tf_op jit(solution)/shard_map/dot_general | solution.py:23
  251.6 4.8 fusion.26
  260.3 6.1 %fusion.72 = bf16[1024,2048]{1,0:T(8,128)(2,1)} fusion(bf16[1024,1024]{0,1:T(8,128)(2,1)S(1)} %copy-done.46, bf16[1024,2048]{1,0:T(8,128)(2,1)S(1)} %multiply_convert_fusion), kind=kOutput, calls=%fused_computation.234 | convolution fusion | flops 4294967296 | bytes 10485760 | tf_op jit(solution)/shard_map/dot_general | solution.py:23
  266.4 2.8 collective-permute-start.16
  271.5 3.7 convert_add_fusion.1
  275.2 4.3 fusion.37.refs_5_
  279.5 27.9 %shard_map.282 = (bf16[1024,512]{1,0:T(8,128)(2,1)S(1)}, bf16[1024,512]{1,0:T(8,128)(2,1)S(1)}, bf16[1024,512]{1,0:T(8,128)(2,1)S(1)}) custom-call(bf16[1024,512]{1,0:T(8,128)(2,1)} %copy-done, bf16[1024,1024]{1,0:T(8,128)(2,1)} %fusion.19.refs_1_.refs_2_, bf16[1024,1024]{1,0:T(8,128)(2,1)} %fusion.19.refs_1_.refs_2_, bf16[1024,512]{1,0:T(8,128)(2,1)} %copy-done.2, ...), custom_call_target="tpu_custom_call" | custom-call | flops 1 | bytes 1024 | tf_op jit(solution)/shard_map/pallas_call | solution.py:218
  307.4 4.0 fusion.42
  325.4 7.1 %reduce-scatter.4.cloned.1.call-done = bf16[128,2048]{1,0:T(8,128)(2,1)} async-done(((bf16[1024,2048]{1,0:T(8,128)(2,1)}), bf16[128,2048]{1,0:T(8,128)(2,1)}) %reduce-scatter.4.cloned.1.call-update) | async-done | bytes 524304 | tf_op jit(solution)/shard_map/reduce_scatter | solution.py:309
  332.5 4.7 broadcast_select_fusion.1
  338.4 4.9 multiply_reduce_fusion.5
  344.3 6.0 %fusion.9 = (f32[1024,1024]{0,1:T(8,128)}, f32[1024,1024]{0,1:T(8,128)S(1)}, f32[1024,1024]{0,1:T(8,128)}) fusion(f32[1024,1024]{0,1:T(8,128)S(1)} %copy-done.11, f32[1024]{0:T(1024)S(1)} %add_rsqrt_fusion.1, f32[1024]{0:T(1024)S(1)} %broadcast_multiply_fusion.5, bf16[1024,1024]{0,1:T(8,128)(2,1)} %collective-permute-done.15, bf16[1024,1024]{0,1:T(8,128)(2,1)} %fusion.42, ...), kind=kLoop, calls=%fused_computation.37 | loop fusion | flops 12582912 | bytes 25186304 | tf_op jit(solution)/shard_map/mul | solution.py:414
  352.7 3.5 fusion.33.refs_5_
  363.7 20.5 %shard_map.283 = (bf16[1024,512]{1,0:T(8,128)(2,1)S(1)}, bf16[1024,512]{1,0:T(8,128)(2,1)S(1)}, bf16[1024,512]{1,0:T(8,128)(2,1)S(1)}) custom-call(bf16[1024,1536]{1,0:T(8,128)(2,1)} %fusion.7.refs_0_.refs_1_.refs_2_, bf16[1024,1536]{1,0:T(8,128)(2,1)} %fusion.7.refs_0_.refs_1_.refs_2_, bf16[1024,1536]{1,0:T(8,128)(2,1)} %fusion.7.refs_0_.refs_1_.refs_2_, ...), custom_call_target="tpu_custom_call" | custom-call | flops 1 | bytes 1024 | tf_op jit(solution)/shard_map/pallas_call | solution.py:218
  385.5 5.2 fusion.62
  394.6 4.6 fusion.5
  404.2 3.1 copy.112
  407.4 6.7 %fusion.21 = bf16[1024,1024]{0,1:T(8,128)(2,1)} fusion(bf16[1024,1024]{1,0:T(8,128)(2,1)} %copy-done.57, bf16[1024,2048]{1,0:T(8,128)(2,1)} %copy-done.40), kind=kOutput, calls=%fused_computation.67 | convolution fusion | flops 2147483648 | bytes 6291456 | tf_op jit(solution)/shard_map/dot_general | solution.py:23
  414.1 5.7 %fusion.74 = bf16[1024,1024]{0,1:T(8,128)(2,1)} fusion(bf16[1024,2048]{1,0:T(8,128)(2,1)S(1)} %copy-done.78, bf16[1024,2048]{1,0:T(8,128)(2,1)S(1)} %copy-done.74), kind=kOutput, calls=%fused_computation.236 | convolution fusion | flops 4294967296 | bytes 10485760 | tf_op jit(solution)/shard_map/dot_general | solution.py:23
  419.8 3.8 broadcast_select_fusion.4
  425.5 10.7 %collective-permute-start.21 = (bf16[512,1024]{0,1:T(8,128)(2,1)S(1)}, bf16[512,1024]{0,1:T(8,128)(2,1)S(1)}, u32[]{:S(2)}, u32[]{:S(2)}) collective-permute-start(bf16[512,1024]{0,1:T(8,128)(2,1)S(1)} %broadcast_select_fusion.8), channel_id=1, source_target_pairs={{0,2},{1,3},{2,0},{3,1},{4,6},{5,7},{6,4},{7,5},{8,10},{9,11},{10,... | collective-permute-start | bytes 3145736 | tf_op jit(solution)/shard_map/ppermute | solution.py:267
  439.5 4.7 collective-permute-start.25
  459.7 4.1 multiply_reduce_fusion.7
  463.9 12.6 %collective-permute-start.32 = (f32[8,1024]{1,0:T(8,128)S(1)}, f32[8,1024]{1,0:T(8,128)S(1)}, u32[]{:S(2)}, u32[]{:S(2)}) collective-permute-start(f32[8,1024]{1,0:T(8,128)S(1)} %stack.31), channel_id=1, source_target_pairs={{0,2},{1,3},{2,0},{3,1},{4,6},{5,7},{6,4},{7,5},{8,10},{9,11},{10,... | collective-permute-start | bytes 98312 | tf_op jit(solution)/shard_map/ppermute | solution.py:267
  476.4 4.6 fusion.12
  483.4 3.1 select_convert_fusion
  495.2 2.8 collective-permute-done.36
  499.7 3.6 collective-permute-start.34
  507.5 3.6 collective-permute-done.34
  519.2 7.7 %reduce-scatter.6.cloned.1.call-done = bf16[64,1536]{1,0:T(8,128)(2,1)} async-done(((bf16[1024,1536]{1,0:T(8,128)(2,1)}), bf16[64,1536]{1,0:T(8,128)(2,1)}) %reduce-scatter.6.cloned.1.call-update) | async-done | bytes 196624 | tf_op jit(solution)/shard_map/reduce_scatter | solution.py:306
  (378 shorter events, 153.7 us)
Async XLA Ops:
  7.2 58.4 %all-gather.5.cloned.1.call-start = ((), (), s32[]{:S(2)}) async-start(), calls=%async_computation.3 | async-start | bytes 4734976 | tf_op jit(solution)/shard_map/all_gather | solution.py:288
  10.6 107.0 %all-gather.7.cloned.1.call-start = ((), (), s32[]{:S(2)}) async-start(), calls=%async_computation.4 | async-start | bytes 4456448 | tf_op jit(solution)/shard_map/all_gather | solution.py:288
  12.4 156.5 %all-gather.9.cloned.1.call-start = ((), (), s32[]{:S(2)}) async-start(), calls=%async_computation.5 | async-start | bytes 4456448 | tf_op jit(solution)/shard_map/all_gather | solution.py:288
  16.2 20.5 %collective-permute-start.2 = (bf16[1024,1024]{0,1:T(8,128)(2,1)}, bf16[1024,1024]{0,1:T(8,128)(2,1)}, u32[]{:S(2)}, u32[]{:S(2)}) collective-permute-start(bf16[1024,1024]{0,1:T(8,128)(2,1)} %pad_maximum_fusion), channel_id=1, source_target_pairs={{1,2},{2,1},{5,6},{6,5},{9,10},{10,9},{13,14},{14,13},{17,18},{18,... | collective-permute-start | bytes 6291464 | tf_op jit(solution)/shard_map/ppermute | solution.py:267
  19.6 15.3 %collective-permute-start = (bf16[512,1024]{0,1:T(8,128)(2,1)S(1)}, bf16[512,1024]{0,1:T(8,128)(2,1)S(1)}, u32[]{:S(2)}, u32[]{:S(2)}) collective-permute-start(bf16[512,1024]{0,1:T(8,128)(2,1)S(1)} %copy.93), channel_id=1, source_target_pairs={{1,2},{2,1},{5,6},{6,5},{9,10},{10,9},{13,14},{14,13},{17,18},{18,... | collective-permute-start | bytes 3145736 | tf_op jit(solution)/shard_map/ppermute | solution.py:267
  20.4 8.6 %collective-permute-start.3 = (bf16[64,2048]{1,0:T(8,128)(2,1)S(1)}, bf16[64,2048]{1,0:T(8,128)(2,1)S(1)}, u32[]{:S(2)}, u32[]{:S(2)}) collective-permute-start(bf16[64,2048]{1,0:T(8,128)(2,1)S(1)} %copy-done.59), channel_id=1, source_target_pairs={{1,2},{2,1},{5,6},{6,5},{9,10},{10,9},{13,14},{14,13},{17,18},{18,... | collective-permute-start | bytes 786440 | tf_op jit(solution)/shard_map/ppermute | solution.py:267
  21.1 13.9 %collective-permute-start.4 = (bf16[64,2048]{1,0:T(8,128)(2,1)S(1)}, bf16[64,2048]{1,0:T(8,128)(2,1)S(1)}, u32[]{:S(2)}, u32[]{:S(2)}) collective-permute-start(bf16[64,2048]{1,0:T(8,128)(2,1)S(1)} %copy-done.59), channel_id=1, source_target_pairs={{0,1},{1,3},{3,2},{2,0},{4,5},{5,7},{7,6},{6,4},{8,9},{9,11},{11,1... | collective-permute-start | bytes 786440 | tf_op jit(solution)/shard_map/ppermute | solution.py:267
  28.3 0.7 collective-permute-start.1
  65.6 52.0 %collective-permute-start.6 = (bf16[1024,2176]{1,0:T(8,128)(2,1)}, bf16[1024,2176]{1,0:T(8,128)(2,1)}, u32[]{:S(2)}, u32[]{:S(2)}) collective-permute-start(bf16[1024,2176]{1,0:T(8,128)(2,1)} %all-gather.5.cloned.1.call-done), channel_id=1, source_target_pairs={{1,2},{2,1},{5,6},{6,5},{9,10},{10,9},{13,14},{14,13},{17,18},{18,... | collective-permute-start | bytes 13369352 | tf_op jit(solution)/shard_map/ppermute | solution.py:267
  68.4 174.4 %all-gather.11.cloned.1.call-start = ((), (), s32[]{:S(2)}) async-start(), calls=%async_computation.6 | async-start | bytes 4718592 | tf_op jit(solution)/shard_map/all_gather | solution.py:303
  69.9 8.5 %collective-permute-start.5 = (bf16[512,1024]{0,1:T(8,128)(2,1)}, bf16[512,1024]{0,1:T(8,128)(2,1)}, u32[]{:S(2)}, u32[]{:S(2)}) collective-permute-start(bf16[512,1024]{0,1:T(8,128)(2,1)} %broadcast_select_fusion.19), channel_id=1, source_target_pairs={{0,2},{1,3},{2,0},{3,1},{4,6},{5,7},{6,4},{7,5},{8,10},{9,11},{10,... | collective-permute-start | bytes 3145736 | tf_op jit(solution)/shard_map/ppermute | solution.py:267
  73.8 4.3 collective-permute-start.7
  75.9 74.6 %collective-permute-start.8 = (bf16[512,1024]{0,1:T(8,128)(2,1)}, bf16[512,1024]{0,1:T(8,128)(2,1)}, u32[]{:S(2)}, u32[]{:S(2)}) collective-permute-start(bf16[512,1024]{0,1:T(8,128)(2,1)} %slice.227), channel_id=1, source_target_pairs={{0,2},{1,3},{2,0},{3,1},{4,6},{5,7},{6,4},{7,5},{8,10},{9,11},{10,... | collective-permute-start | bytes 3145736 | tf_op jit(solution)/shard_map/ppermute | solution.py:267
  81.1 44.5 %copy-start.64 = (f32[1024]{0:T(1024)}, f32[1024]{0:T(1024)S(1)}, u32[]{:S(2)}) copy-start(f32[1024]{0:T(1024)S(1)} %broadcast_multiply_fusion.6) | copy-start | bytes 12292
  117.6 54.1 %collective-permute-start.10 = (bf16[1024,2048]{1,0:T(8,128)(2,1)}, bf16[1024,2048]{1,0:T(8,128)(2,1)}, u32[]{:S(2)}, u32[]{:S(2)}) collective-permute-start(bf16[1024,2048]{1,0:T(8,128)(2,1)} %all-gather.7.cloned.1.call-done), channel_id=1, source_target_pairs={{1,2},{2,1},{5,6},{6,5},{9,10},{10,9},{13,14},{14,13},{17,18},{18,... | collective-permute-start | bytes 12582920 | tf_op jit(solution)/shard_map/ppermute | solution.py:267
  146.0 204.3 %copy-start.4 = (bf16[1024,512]{1,0:T(8,128)(2,1)}, bf16[1024,512]{1,0:T(8,128)(2,1)S(1)}, u32[]{:S(2)}) copy-start(bf16[1024,512]{1,0:T(8,128)(2,1)S(1)} %get-tuple-element.73.refs_3_) | copy-start | bytes 3145732
  148.7 11.1 %collective-permute-start.9 = (bf16[1024,1024]{0,1:T(8,128)(2,1)}, bf16[1024,1024]{0,1:T(8,128)(2,1)}, u32[]{:S(2)}, u32[]{:S(2)}) collective-permute-start(bf16[1024,1024]{0,1:T(8,128)(2,1)} %fusion.47), channel_id=1, source_target_pairs={{0,2},{1,3},{2,0},{3,1},{4,6},{5,7},{6,4},{7,5},{8,10},{9,11},{10,... | collective-permute-start | bytes 6291464 | tf_op jit(solution)/shard_map/ppermute | solution.py:267
  153.6 3.2 collective-permute-start.11
  155.1 177.3 %reduce-scatter.4.cloned.1.call-start = ((), (), s32[]{:S(2)}) async-start(), calls=%async_computation.7 | async-start | bytes 4718592 | tf_op jit(solution)/shard_map/reduce_scatter | solution.py:309
  168.9 44.0 %collective-permute-start.13 = (bf16[1024,2048]{1,0:T(8,128)(2,1)}, bf16[1024,2048]{1,0:T(8,128)(2,1)}, u32[]{:S(2)}, u32[]{:S(2)}) collective-permute-start(bf16[1024,2048]{1,0:T(8,128)(2,1)} %all-gather.9.cloned.1.call-done), channel_id=1, source_target_pairs={{1,2},{2,1},{5,6},{6,5},{9,10},{10,9},{13,14},{14,13},{17,18},{18,... | collective-permute-start | bytes 12582920 | tf_op jit(solution)/shard_map/ppermute | solution.py:267
  201.2 4.9 collective-permute-start.12
  242.8 274.6 %reduce-scatter.8.cloned.1.call-start = ((), (), s32[]{:S(2)}) async-start(), calls=%async_computation.9 | async-start | bytes 4456448 | tf_op jit(solution)/shard_map/reduce_scatter | solution.py:306
  256.4 12.8 %collective-permute-start.14 = (bf16[1024,1024]{0,1:T(8,128)(2,1)S(1)}, bf16[1024,1024]{0,1:T(8,128)(2,1)S(1)}, u32[]{:S(2)}, u32[]{:S(2)}) collective-permute-start(bf16[1024,1024]{0,1:T(8,128)(2,1)S(1)} %fusion.26), channel_id=1, source_target_pairs={{0,2},{1,3},{2,0},{3,1},{4,6},{5,7},{6,4},{7,5},{8,10},{9,11},{10,... | collective-permute-start | bytes 6291464 | tf_op jit(solution)/shard_map/ppermute | solution.py:267
  266.4 59.0 %collective-permute-start.16 = (bf16[1024,2048]{1,0:T(8,128)(2,1)}, bf16[1024,2048]{1,0:T(8,128)(2,1)}, u32[]{:S(2)}, u32[]{:S(2)}) collective-permute-start(bf16[1024,2048]{1,0:T(8,128)(2,1)} %fusion.72), channel_id=1, source_target_pairs={{1,2},{2,1},{5,6},{6,5},{9,10},{10,9},{13,14},{14,13},{17,18},{18,... | collective-permute-start | bytes 12582920 | tf_op jit(solution)/shard_map/ppermute | solution.py:267
  311.4 27.1 %collective-permute-start.15 = (bf16[1024,1024]{0,1:T(8,128)(2,1)}, bf16[1024,1024]{0,1:T(8,128)(2,1)}, u32[]{:S(2)}, u32[]{:S(2)}) collective-permute-start(bf16[1024,1024]{0,1:T(8,128)(2,1)} %fusion.42), channel_id=1, source_target_pairs={{0,2},{1,3},{2,0},{3,1},{4,6},{5,7},{6,4},{7,5},{8,10},{9,11},{10,... | collective-permute-start | bytes 6291464 | tf_op jit(solution)/shard_map/ppermute | solution.py:267
  356.3 170.6 %reduce-scatter.6.cloned.1.call-start = ((), (), s32[]{:S(2)}) async-start(), calls=%async_computation.8 | async-start | bytes 3342336 | tf_op jit(solution)/shard_map/reduce_scatter | solution.py:306
  358.6 40.6 %collective-permute-start.18 = (bf16[2,2,2,64,1280]{4,3,1,0,2:T(8,128)(2,1)S(1)}, bf16[2,2,2,64,1280]{4,3,1,0,2:T(8,128)(2,1)S(1)}, u32[]{:S(2)}, u32[]{:S(2)}) collective-permute-start(bf16[2,2,2,64,1280]{4,3,1,0,2:T(8,128)(2,1)S(1)} %pad_maximum_fusion.6), channel_id=1, source_target_pairs={{1,2},{2,1},{5,6},{6,5},{9,10},{10,9},{13,14},{14,13},{17,18},{18,... | collective-permute-start | bytes 3932168 | tf_op jit(solution)/shard_map/ppermute | solution.py:267
  359.6 39.6 %collective-permute-start.20 = (bf16[2,2,2,64,1280]{4,3,2,1,0:T(8,128)(2,1)S(1)}, bf16[2,2,2,64,1280]{4,3,2,1,0:T(8,128)(2,1)S(1)}, u32[]{:S(2)}, u32[]{:S(2)}) collective-permute-start(bf16[2,2,2,64,1280]{4,3,2,1,0:T(8,128)(2,1)S(1)} %pad_maximum_fusion.8), channel_id=1, source_target_pairs={{0,4},{1,5},{2,6},{3,7},{4,0},{5,1},{6,2},{7,3},{8,12},{9,13},{10,... | collective-permute-start | bytes 3932168 | tf_op jit(solution)/shard_map/ppermute | solution.py:267
  361.2 38.0 %collective-permute-start.19 = (bf16[2,2,2,64,1280]{4,3,1,0,2:T(8,128)(2,1)S(1)}, bf16[2,2,2,64,1280]{4,3,1,0,2:T(8,128)(2,1)S(1)}, u32[]{:S(2)}, u32[]{:S(2)}) collective-permute-start(bf16[2,2,2,64,1280]{4,3,1,0,2:T(8,128)(2,1)S(1)} %pad_maximum_fusion.7), channel_id=1, source_target_pairs={{1,0},{3,1},{2,3},{0,2},{5,4},{7,5},{6,7},{4,6},{9,8},{11,9},{10,1... | collective-permute-start | bytes 3932168 | tf_op jit(solution)/shard_map/ppermute | solution.py:267
  391.0 28.9 %collective-permute-start.17 = (bf16[1024,1536]{1,0:T(8,128)(2,1)}, bf16[1024,1536]{1,0:T(8,128)(2,1)}, u32[]{:S(2)}, u32[]{:S(2)}) collective-permute-start(bf16[1024,1536]{1,0:T(8,128)(2,1)} %fusion.62), channel_id=1, source_target_pairs={{1,2},{2,1},{5,6},{6,5},{9,10},{10,9},{13,14},{14,13},{17,18},{18,... | collective-permute-start | bytes 9437192 | tf_op jit(solution)/shard_map/ppermute | solution.py:267
  400.8 37.0 %collective-permute-start.26 = (bf16[2,2,64,1280]{3,2,1,0:T(8,128)(2,1)}, bf16[2,2,64,1280]{3,2,1,0:T(8,128)(2,1)}, u32[]{:S(2)}, u32[]{:S(2)}) collective-permute-start(bf16[2,2,64,1280]{3,2,1,0:T(8,128)(2,1)} %dynamic-slice_bitcast_fusion.4), channel_id=1, source_target_pairs={{0,4},{1,5},{2,6},{3,7},{4,0},{5,1},{6,2},{7,3},{8,12},{9,13},{10,... | collective-permute-start | bytes 1966088 | tf_op jit(solution)/shard_map/ppermute | solution.py:267
  402.7 35.2 %collective-permute-start.28 = (bf16[2,2,64,1280]{3,2,1,0:T(8,128)(2,1)}, bf16[2,2,64,1280]{3,2,1,0:T(8,128)(2,1)}, u32[]{:S(2)}, u32[]{:S(2)}) collective-permute-start(bf16[2,2,64,1280]{3,2,1,0:T(8,128)(2,1)} %get-tuple-element.206), channel_id=1, source_target_pairs={{1,0},{3,1},{2,3},{0,2},{5,4},{7,5},{6,7},{4,6},{9,8},{11,9},{10,1... | collective-permute-start | bytes 1966088 | tf_op jit(solution)/shard_map/ppermute | solution.py:267
  402.7 36.7 %collective-permute-start.27 = (bf16[2,2,64,1280]{3,2,1,0:T(8,128)(2,1)S(1)}, bf16[2,2,64,1280]{3,2,1,0:T(8,128)(2,1)}, u32[]{:S(2)}, u32[]{:S(2)}) collective-permute-start(bf16[2,2,64,1280]{3,2,1,0:T(8,128)(2,1)S(1)} %get-tuple-element.207), channel_id=1, source_target_pairs={{1,2},{2,1},{5,6},{6,5},{9,10},{10,9},{13,14},{14,13},{17,18},{18,... | collective-permute-start | bytes 1966088 | tf_op jit(solution)/shard_map/ppermute | solution.py:267
  425.5 20.9 %collective-permute-start.21 = (bf16[512,1024]{0,1:T(8,128)(2,1)S(1)}, bf16[512,1024]{0,1:T(8,128)(2,1)S(1)}, u32[]{:S(2)}, u32[]{:S(2)}) collective-permute-start(bf16[512,1024]{0,1:T(8,128)(2,1)S(1)} %broadcast_select_fusion.8), channel_id=1, source_target_pairs={{0,2},{1,3},{2,0},{3,1},{4,6},{5,7},{6,4},{7,5},{8,10},{9,11},{10,... | collective-permute-start | bytes 3145736 | tf_op jit(solution)/shard_map/ppermute | solution.py:267
  436.3 13.6 %collective-permute-start.23 = (bf16[512,1024]{0,1:T(8,128)(2,1)S(1)}, bf16[512,1024]{0,1:T(8,128)(2,1)S(1)}, u32[]{:S(2)}, u32[]{:S(2)}) collective-permute-start(bf16[512,1024]{0,1:T(8,128)(2,1)S(1)} %broadcast_select_fusion.9), channel_id=1, source_target_pairs={{0,2},{1,3},{2,0},{3,1},{4,6},{5,7},{6,4},{7,5},{8,10},{9,11},{10,... | collective-permute-start | bytes 3145736 | tf_op jit(solution)/shard_map/ppermute | solution.py:267
  437.8 52.8 %collective-permute-start.31 = (bf16[64,2048]{1,0:T(8,128)(2,1)S(1)}, bf16[64,2048]{1,0:T(8,128)(2,1)}, u32[]{:S(2)}, u32[]{:S(2)}) collective-permute-start(bf16[64,2048]{1,0:T(8,128)(2,1)S(1)} %copy-done.58), channel_id=1, source_target_pairs={{1,0},{3,1},{2,3},{0,2},{5,4},{7,5},{6,7},{4,6},{9,8},{11,9},{10,1... | collective-permute-start | bytes 786440 | tf_op jit(solution)/shard_map/ppermute | solution.py:267
  438.0 52.7 %collective-permute-start.30 = (bf16[64,2048]{1,0:T(8,128)(2,1)S(1)}, bf16[64,2048]{1,0:T(8,128)(2,1)}, u32[]{:S(2)}, u32[]{:S(2)}) collective-permute-start(bf16[64,2048]{1,0:T(8,128)(2,1)S(1)} %get-tuple-element.223), channel_id=1, source_target_pairs={{1,2},{2,1},{5,6},{6,5},{9,10},{10,9},{13,14},{14,13},{17,18},{18,... | collective-permute-start | bytes 786440 | tf_op jit(solution)/shard_map/ppermute | solution.py:267
  439.5 18.0 %collective-permute-start.25 = (bf16[512,1024]{0,1:T(8,128)(2,1)}, bf16[512,1024]{0,1:T(8,128)(2,1)}, u32[]{:S(2)}, u32[]{:S(2)}) collective-permute-start(bf16[512,1024]{0,1:T(8,128)(2,1)} %broadcast_select_fusion.10), channel_id=1, source_target_pairs={{0,2},{1,3},{2,0},{3,1},{4,6},{5,7},{6,4},{7,5},{8,10},{9,11},{10,... | collective-permute-start | bytes 3145736 | tf_op jit(solution)/shard_map/ppermute | solution.py:267
  448.2 15.7 %collective-permute-start.22 = (bf16[512,1024]{0,1:T(8,128)(2,1)}, bf16[512,1024]{0,1:T(8,128)(2,1)}, u32[]{:S(2)}, u32[]{:S(2)}) collective-permute-start(bf16[512,1024]{0,1:T(8,128)(2,1)} %fusion.18), channel_id=1, source_target_pairs={{1,2},{2,1},{5,6},{6,5},{9,10},{10,9},{13,14},{14,13},{17,18},{18,... | collective-permute-start | bytes 3145736 | tf_op jit(solution)/shard_map/ppermute | solution.py:267
  451.3 12.6 %collective-permute-start.24 = (bf16[512,1024]{0,1:T(8,128)(2,1)}, bf16[512,1024]{0,1:T(8,128)(2,1)}, u32[]{:S(2)}, u32[]{:S(2)}) collective-permute-start(bf16[512,1024]{0,1:T(8,128)(2,1)} %add_convert_fusion.5), channel_id=1, source_target_pairs={{1,2},{2,1},{5,6},{6,5},{9,10},{10,9},{13,14},{14,13},{17,18},{18,... | collective-permute-start | bytes 3145736 | tf_op jit(solution)/shard_map/ppermute | solution.py:267
  457.5 35.2 %collective-permute-start.29 = (bf16[2,64,2560]{2,1,0:T(8,128)(2,1)}, bf16[2,64,2560]{2,1,0:T(8,128)(2,1)}, u32[]{:S(2)}, u32[]{:S(2)}) collective-permute-start(bf16[2,64,2560]{2,1,0:T(8,128)(2,1)} %fusion.50), channel_id=1, source_target_pairs={{0,16},{1,17},{2,18},{3,19},{4,20},{5,21},{6,22},{7,23},{8,24},{9,... | collective-permute-start | bytes 1966088 | tf_op jit(solution)/shard_map/ppermute | solution.py:267
  463.9 18.9 %collective-permute-start.32 = (f32[8,1024]{1,0:T(8,128)S(1)}, f32[8,1024]{1,0:T(8,128)S(1)}, u32[]{:S(2)}, u32[]{:S(2)}) collective-permute-start(f32[8,1024]{1,0:T(8,128)S(1)} %stack.31), channel_id=1, source_target_pairs={{0,2},{1,3},{2,0},{3,1},{4,6},{5,7},{6,4},{7,5},{8,10},{9,11},{10,... | collective-permute-start | bytes 98312 | tf_op jit(solution)/shard_map/ppermute | solution.py:267
  481.1 26.4 %collective-permute-start.35 = (bf16[512,1024]{0,1:T(8,128)(2,1)}, bf16[512,1024]{0,1:T(8,128)(2,1)}, u32[]{:S(2)}, u32[]{:S(2)}) collective-permute-start(bf16[512,1024]{0,1:T(8,128)(2,1)} %fusion.12), channel_id=1, source_target_pairs={{1,2},{2,1},{5,6},{6,5},{9,10},{10,9},{13,14},{14,13},{17,18},{18,... | collective-permute-start | bytes 3145736 | tf_op jit(solution)/shard_map/ppermute | solution.py:267
  482.8 7.9 %collective-permute-start.33 = (f32[8,1024]{1,0:T(8,128)S(1)}, f32[8,1024]{1,0:T(8,128)S(1)}, u32[]{:S(2)}, u32[]{:S(2)}) collective-permute-start(f32[8,1024]{1,0:T(8,128)S(1)} %add.264), channel_id=1, source_target_pairs={{0,4},{1,5},{2,6},{3,7},{4,0},{5,1},{6,2},{7,3},{8,12},{9,13},{10,... | collective-permute-start | bytes 98312 | tf_op jit(solution)/shard_map/ppermute | solution.py:267
  492.7 5.3 collective-permute-start.36
  498.0 5.5 %collective-permute-start.37 = (f32[8,1024]{1,0:T(8,128)S(1)}, f32[8,1024]{1,0:T(8,128)S(1)}, u32[]{:S(2)}, u32[]{:S(2)}) collective-permute-start(f32[8,1024]{1,0:T(8,128)S(1)} %add.269), channel_id=1, source_target_pairs={{0,16},{1,17},{2,18},{3,19},{4,20},{5,21},{6,22},{7,23},{8,24},{9,... | collective-permute-start | bytes 98312 | tf_op jit(solution)/shard_map/ppermute | solution.py:267
  499.7 11.4 %collective-permute-start.34 = (bf16[64,2560]{1,0:T(8,128)(2,1)S(1)}, bf16[64,2560]{1,0:T(8,128)(2,1)S(1)}, u32[]{:S(2)}, u32[]{:S(2)}) collective-permute-start(bf16[64,2560]{1,0:T(8,128)(2,1)S(1)} %dynamic-slice_bitcast_fusion.5), channel_id=1, source_target_pairs={{0,8},{1,9},{2,10},{3,11},{4,12},{5,13},{6,14},{7,15},{8,0},{9,1},... | collective-permute-start | bytes 983048 | tf_op jit(solution)/shard_map/ppermute | solution.py:267
  503.6 3.9 collective-permute-start.38
  (79 other events, 521.2 us)
Sparse Core Ops, SparseCore 0:
  10.9 54.6 all-gather.4
  68.3 49.2 all-gather.6
  119.8 49.0 all-gather.8
  170.8 71.8 all-gather.10
  246.3 86.1 reduce-scatter.3
  356.4 76.0 reduce-scatter.7
  455.8 71.0 reduce-scatter.5

commit v2 on v1

--- a/solution.py
+++ b/solution.py
@@ -97,7 +97,7 @@
         lse_ref[start : start + block, :] = jnp.where(lane < HEAD_DIM, sums[0], sums[1])
 
 
-def attention(q, k, v, offsets, pairs, bits, block=256):
+def attention(q, k, v, offsets, pairs, bits, block=512):
     tokens = q.shape[0]
     tree = bits is not None
 
@@ -158,10 +158,16 @@
         preferred_element_type=F32,
     )
     lse_rows = jnp.transpose(lse_ref[...])
+    keys_across = jnp.transpose(k_ref[...].astype(F32)).astype(BF)
+    row = lax.broadcasted_iota(jnp.int32, keys_across.shape, 0)
+    zero = jnp.zeros_like(keys_across)
+    keys_across = (
+        jnp.where(row < HEAD_DIM, keys_across, zero),
+        jnp.where(row >= HEAD_DIM, keys_across, zero),
+    )
     for start in range(0, keys, block):
         first = start if tree else 0
         key_rows = k_ref[start : start + block, :]
-        key_masked = head_masks(key_rows)
         value_rows = v_ref[start : start + block, :]
         dv = None
         dk = None
@@ -181,7 +187,7 @@
             weight_grad = mm_rt(value_rows, grads[side][first:, :])
             score_grad = (weights * (weight_grad - delta[side : side + 1, first:])).astype(BF)
             dk_part = mm(score_grad, queries[side][first:, :])
-            dq_part = mm_lt(score_grad, key_masked[side])
+            dq_part = mm(keys_across[side][:, start : start + block], score_grad)
             dv = dv_part if dv is None else dv + dv_part
             dk = dk_part if dk is None else dk + dk_part
             dq = dq_part if dq is None else dq + dq_part
@@ -190,14 +196,15 @@
         if start == 0:
             dq_acc[...] = dq
         else:
-            dq_acc[first:, :] += dq
-    dq_ref[...] = (dq_acc[...] * scale).astype(BF)
-
-
-def attention_back(q, k, v, o, lse, do, offsets, pairs, bits, block=256):
+            dq_acc[:, first:] += dq
+    dq_ref[...] = (jnp.transpose(dq_acc[...]) * scale).astype(BF)
+
+
+def attention_back(q, k, v, o, lse, do, offsets, pairs, bits):
     tokens = q.shape[0]
     keys = k.shape[0]
     tree = bits is not None
+    block = 256 if tree else 512
 
     def spec(rows, shift):
         return pl.BlockSpec((rows, PAIR), lambda i, shift=shift: (0, i + shift))
@@ -207,7 +214,7 @@
         spec(tokens, 0), spec(tokens, 0), spec(tokens, 0),
     ]
     operands = [q, k, v, o, lse, do]
-    scratch = [pltpu.VMEM((tokens, PAIR), F32)]
+    scratch = [pltpu.VMEM((PAIR, tokens), F32)]
     if tree:
         in_specs += [
             pl.BlockSpec((1, tokens), lambda i: (0, 0)),

time: 542 us -> 540 us (level)
  Pallas kernels: 82.5 us -> 76 us
  transfers between devices with their start and end apart: 46 -> 46, of which waited for: 14 -> 13; matrix products, arithmetic and copies ran while one was open for 37% -> 38% of each run, Pallas kernels for 15% -> 14%
where the time goes in v2:
time: 540 us; the launch traced here: 534 us
  waiting for transfers between devices  117 us (22%)
  other arithmetic  97.7 us (18%)
  matrix products  92 us (17%)
  starting transfers between devices  88.8 us (16%)
  Pallas kernels  76 us (14%)
  local copies, waits for them, and re-layouts  47.2 us (9%)
  between operations  15.6 us (3%)
    dot_general x21, matrix products, dot(): lax.dot_general(former, latter, (dims, ((), ())), preferred_element_type=...  92 us
    ppermute x39, starting transfers between devices, send(): return lax.ppermute(values, AXES, pairs)  88.3 us
    all_gather x3, waiting for transfers between devices, gather(): return lax.all_gather(shard, 'dp', axis=0, tiled=True)  68 us
    pallas_call x2, Pallas kernels, attention_back(): pl.pallas_call(functools.partial(attention_back_kernel, tree, block), gri...  46.8 us
    pallas_call x2, Pallas kernels, attention(): pl.pallas_call(functools.partial(attention_kernel, tree, block), grid=(pa...  29.2 us
    unnamed x173, local copies, waits for them, and re-layouts  25.9 us
    ppermute x39, waiting for transfers between devices, send(): return lax.ppermute(values, AXES, pairs)  21.7 us
    select_n x7, other arithmetic, cross(): jnp.where(self.home, values, got)  15.9 us
  transfers between devices with their start and end apart: 46, of which 13 were waited for; matrix products, arithmetic and copies ran while one was open for 38% of the time, Pallas kernels for 14%

profile of v2, /device:TPU:0, one launch (start us, length us, event | category | flops | bytes accessed | tf_op | source)
XLA Modules:
  0.0 534.3 jit_solution(5001131589763955072)
XLA Ops:
  21.1 7.1 %collective-permute-start.4 = (bf16[64,2048]{1,0:T(8,128)(2,1)S(1)}, bf16[64,2048]{1,0:T(8,128)(2,1)S(1)}, u32[]{:S(2)}, u32[]{:S(2)}) collective-permute-start(bf16[64,2048]{1,0:T(8,128)(2,1)S(1)} %copy-done.59), channel_id=1, source_target_pairs={{0,1},{1,3},{3,2},{2,0},{4,5},{5,7},{7,6},{6,4},{8,9},{9,11},{11,1... | collective-permute-start | bytes 786440 | tf_op jit(solution)/shard_map/ppermute | solution.py:274
  29.0 6.0 %collective-permute-done.4 = bf16[64,2048]{1,0:T(8,128)(2,1)S(1)} collective-permute-done((bf16[64,2048]{1,0:T(8,128)(2,1)S(1)}, bf16[64,2048]{1,0:T(8,128)(2,1)S(1)}, u32[]{:S(2)}, u32[]{:S(2)}) %collective-permute-start.4) | collective-permute-done | bytes 262176 | tf_op jit(solution)/shard_map/ppermute | solution.py:274
  36.6 28.9 %all-gather.5.cloned.1.call-done = bf16[1024,2176]{1,0:T(8,128)(2,1)} async-done(((bf16[64,2176]{1,0:T(8,128)(2,1)}), bf16[1024,2176]{1,0:T(8,128)(2,1)}) %all-gather.5.cloned.1.call-update) | async-done | bytes 4456464 | tf_op jit(solution)/shard_map/all_gather | solution.py:295
  81.7 35.9 %all-gather.7.cloned.1.call-done = bf16[1024,2048]{1,0:T(8,128)(2,1)} async-done(((bf16[64,2048]{1,0:T(8,128)(2,1)}), bf16[1024,2048]{1,0:T(8,128)(2,1)}) %all-gather.7.cloned.1.call-update) | async-done | bytes 4194320 | tf_op jit(solution)/shard_map/all_gather | solution.py:295
  125.6 5.4 %fusion.7.refs_0_.refs_1_.refs_2_ = bf16[1024,1536]{1,0:T(8,128)(2,1)} fusion(bf16[1024,2176]{1,0:T(8,128)(2,1)S(1)} %broadcast_select_fusion, f32[1024]{0:T(1024)S(1)} %get-tuple-element.230, f32[1024]{0:T(1024)S(1)} %get-tuple-element.234, f32[1024]{0:T(1024)S(1)} %add_rsqrt_fusion.2, f32[1024]{0:T(1024)S(1)} %broadcast_multiply_fusion.6, ...), kind=kOutput, calls=%fused_computation.35 | convolution fusion | flops 3230662656 | bytes 8404992 | tf_op jit(solution)/shard_map/dot_general | solution.py:23
  131.0 13.2 %shard_map.280 = (bf16[1024,512]{1,0:T(8,128)(2,1)S(1)}, f32[1024,512]{1,0:T(8,128)S(1)}) custom-call(bf16[1024,1536]{1,0:T(8,128)(2,1)} %fusion.7.refs_0_.refs_1_.refs_2_, bf16[1024,1536]{1,0:T(8,128)(2,1)} %fusion.7.refs_0_.refs_1_.refs_2_, bf16[1024,1536]{1,0:T(8,128)(2,1)} %fusion.7.refs_0_.refs_1_.refs_2_, s32[1024,1]{1,0:T(8,128)S(1)} %copy.94.refs_3_, ...), custom_call_target="tpu_custom_call" | custom-call | flops 1 | bytes 1024 | tf_op jit(solution)/shard_map/pallas_call | solution.py:117
  148.7 3.1 broadcast_select_fusion.15
  155.0 3.0 broadcast_select_fusion.13
  158.0 3.6 fusion.65
  165.7 3.2 all-gather.9.cloned.1.call-done
  168.9 2.9 collective-permute-start.13
  174.4 3.7 fusion.19.refs_1_.refs_2_
  179.4 15.9 %shard_map.281 = (bf16[1024,512]{1,0:T(8,128)(2,1)S(1)}, f32[1024,512]{1,0:T(8,128)}) custom-call(bf16[1024,512]{1,0:T(8,128)(2,1)S(1)} %fusion.44.refs_0_, bf16[1024,1024]{1,0:T(8,128)(2,1)} %fusion.19.refs_1_.refs_2_, bf16[1024,1024]{1,0:T(8,128)(2,1)} %fusion.19.refs_1_.refs_2_), custom_call_target="tpu_custom_call" | custom-call | flops 1 | bytes 1024 | tf_op jit(solution)/shard_map/pallas_call | solution.py:117
  199.0 3.9 collective-permute-done.12
  202.9 4.8 fusion.64
  212.2 9.3 %fusion.4 = (bf16[1024,2048]{1,0:T(8,128)(2,1)}, bf16[1024,2048]{1,0:T(8,128)(2,1)S(1)}) fusion(bf16[1024,1024]{0,1:T(8,128)(2,1)S(1)} %add_convert_fusion, bf16[1024,2048]{1,0:T(8,128)(2,1)S(1)} %copy-done.75, bf16[1024,2048]{1,0:T(8,128)(2,1)} %collective-permute-done.13, pred[]{:T(512)S(6)} %eq.91), kind=kOutput, calls=%fused_computation.5 | convolution fusion | flops 4320133120 | bytes 18874368 | tf_op jit(solution)/shard_map/dot_general | solution.py:23
  223.5 6.1 %fusion.53 = bf16[1024,2048]{1,0:T(8,128)(2,1)} fusion(bf16[1024,2048]{1,0:T(8,128)(2,1)S(1)} %get-tuple-element.96, bf16[512,1024]{0,1:T(8,128)(2,1)S(1)} %copy-done.37, bf16[512,1024]{0,1:T(8,128)(2,1)S(1)} %copy-done.35), kind=kOutput, calls=%fused_computation.131 | convolution fusion | flops 4299161600 | bytes 10485760 | tf_op jit(solution)/shard_map/dot_general | solution.py:23
  229.6 13.1 %all-gather.11.cloned.1.call-done = bf16[1024,2048]{1,0:T(8,128)(2,1)} async-done(((bf16[128,2048]{1,0:T(8,128)(2,1)}), bf16[1024,2048]{1,0:T(8,128)(2,1)}) %all-gather.11.cloned.1.call-update) | async-done | bytes 4194320 | tf_op jit(solution)/shard_map/all_gather | solution.py:310
  242.8 8.7 %multiply_convert_fusion = bf16[1024,2048]{1,0:T(8,128)(2,1)S(1)} fusion(bf16[1024,2048]{1,0:T(8,128)(2,1)} %get-tuple-element.85, bf16[1024,2048]{1,0:T(8,128)(2,1)} %all-gather.11.cloned.1.call-done, bf16[512,1024]{0,1:T(8,128)(2,1)} %get-tuple-element.198, bf16[512,1024]{0,1:T(8,128)(2,1)} %get-tuple-element.197), kind=kOutput, calls=%fused_computation.6 | convolution fusion | flops 4305453056 | bytes 14680064 | tf_op jit(solution)/shard_map/dot_general | solution.py:23
  251.6 4.8 fusion.26
  260.3 6.1 %fusion.72 = bf16[1024,2048]{1,0:T(8,128)(2,1)} fusion(bf16[1024,1024]{0,1:T(8,128)(2,1)S(1)} %copy-done.46, bf16[1024,2048]{1,0:T(8,128)(2,1)S(1)} %multiply_convert_fusion), kind=kOutput, calls=%fused_computation.234 | convolution fusion | flops 4294967296 | bytes 10485760 | tf_op jit(solution)/shard_map/dot_general | solution.py:23
  266.4 2.8 collective-permute-start.16
  271.5 3.7 convert_add_fusion.1
  275.2 4.3 fusion.37.refs_5_
  279.5 27.6 %shard_map.282 = (bf16[1024,512]{1,0:T(8,128)(2,1)S(1)}, bf16[1024,512]{1,0:T(8,128)(2,1)S(1)}, bf16[1024,512]{1,0:T(8,128)(2,1)S(1)}) custom-call(bf16[1024,512]{1,0:T(8,128)(2,1)} %copy-done, bf16[1024,1024]{1,0:T(8,128)(2,1)} %fusion.19.refs_1_.refs_2_, bf16[1024,1024]{1,0:T(8,128)(2,1)} %fusion.19.refs_1_.refs_2_, bf16[1024,512]{1,0:T(8,128)(2,1)} %copy-done.2, ...), custom_call_target="tpu_custom_call" | custom-call | flops 1 | bytes 1024 | tf_op jit(solution)/shard_map/pallas_call | solution.py:225
  307.1 4.0 fusion.42
  325.1 7.4 %reduce-scatter.4.cloned.1.call-done = bf16[128,2048]{1,0:T(8,128)(2,1)} async-done(((bf16[1024,2048]{1,0:T(8,128)(2,1)}), bf16[128,2048]{1,0:T(8,128)(2,1)}) %reduce-scatter.4.cloned.1.call-update) | async-done | bytes 524304 | tf_op jit(solution)/shard_map/reduce_scatter | solution.py:316
  332.4 4.7 broadcast_select_fusion.1
  338.4 4.9 multiply_reduce_fusion.5
  344.3 6.0 %fusion.9 = (f32[1024,1024]{0,1:T(8,128)}, f32[1024,1024]{0,1:T(8,128)S(1)}, f32[1024,1024]{0,1:T(8,128)}) fusion(f32[1024,1024]{0,1:T(8,128)S(1)} %copy-done.11, f32[1024]{0:T(1024)S(1)} %add_rsqrt_fusion.1, f32[1024]{0:T(1024)S(1)} %broadcast_multiply_fusion.5, bf16[1024,1024]{0,1:T(8,128)(2,1)} %collective-permute-done.15, bf16[1024,1024]{0,1:T(8,128)(2,1)} %fusion.42, ...), kind=kLoop, calls=%fused_computation.37 | loop fusion | flops 12582912 | bytes 25186304 | tf_op jit(solution)/shard_map/mul | solution.py:421
  352.7 3.5 fusion.33.refs_5_
  363.7 19.3 %shard_map.283 = (bf16[1024,512]{1,0:T(8,128)(2,1)S(1)}, bf16[1024,512]{1,0:T(8,128)(2,1)S(1)}, bf16[1024,512]{1,0:T(8,128)(2,1)S(1)}) custom-call(bf16[1024,1536]{1,0:T(8,128)(2,1)} %fusion.7.refs_0_.refs_1_.refs_2_, bf16[1024,1536]{1,0:T(8,128)(2,1)} %fusion.7.refs_0_.refs_1_.refs_2_, bf16[1024,1536]{1,0:T(8,128)(2,1)} %fusion.7.refs_0_.refs_1_.refs_2_, ...), custom_call_target="tpu_custom_call" | custom-call | flops 1 | bytes 1024 | tf_op jit(solution)/shard_map/pallas_call | solution.py:225
  384.2 5.2 fusion.62
  393.3 4.6 fusion.5
  403.0 3.1 copy.112
  406.1 6.7 %fusion.21 = bf16[1024,1024]{0,1:T(8,128)(2,1)} fusion(bf16[1024,1024]{1,0:T(8,128)(2,1)} %copy-done.57, bf16[1024,2048]{1,0:T(8,128)(2,1)} %copy-done.40), kind=kOutput, calls=%fused_computation.67 | convolution fusion | flops 2147483648 | bytes 6291456 | tf_op jit(solution)/shard_map/dot_general | solution.py:23
  412.8 5.7 %fusion.74 = bf16[1024,1024]{0,1:T(8,128)(2,1)} fusion(bf16[1024,2048]{1,0:T(8,128)(2,1)S(1)} %copy-done.78, bf16[1024,2048]{1,0:T(8,128)(2,1)S(1)} %copy-done.74), kind=kOutput, calls=%fused_computation.236 | convolution fusion | flops 4294967296 | bytes 10485760 | tf_op jit(solution)/shard_map/dot_general | solution.py:23
  418.6 3.9 broadcast_select_fusion.4
  424.2 10.4 %collective-permute-start.21 = (bf16[512,1024]{0,1:T(8,128)(2,1)S(1)}, bf16[512,1024]{0,1:T(8,128)(2,1)S(1)}, u32[]{:S(2)}, u32[]{:S(2)}) collective-permute-start(bf16[512,1024]{0,1:T(8,128)(2,1)S(1)} %broadcast_select_fusion.8), channel_id=1, source_target_pairs={{0,2},{1,3},{2,0},{3,1},{4,6},{5,7},{6,4},{7,5},{8,10},{9,11},{10,... | collective-permute-start | bytes 3145736 | tf_op jit(solution)/shard_map/ppermute | solution.py:274
  438.0 5.0 collective-permute-start.25
  458.4 4.1 multiply_reduce_fusion.7
  462.6 12.6 %collective-permute-start.32 = (f32[8,1024]{1,0:T(8,128)S(1)}, f32[8,1024]{1,0:T(8,128)S(1)}, u32[]{:S(2)}, u32[]{:S(2)}) collective-permute-start(f32[8,1024]{1,0:T(8,128)S(1)} %stack.31), channel_id=1, source_target_pairs={{0,2},{1,3},{2,0},{3,1},{4,6},{5,7},{6,4},{7,5},{8,10},{9,11},{10,... | collective-permute-start | bytes 98312 | tf_op jit(solution)/shard_map/ppermute | solution.py:274
  475.2 4.6 fusion.12
  482.2 3.1 select_convert_fusion
  493.9 2.8 collective-permute-done.36
  498.5 4.3 collective-permute-start.34
  507.0 3.7 collective-permute-done.34
  518.9 6.7 %reduce-scatter.6.cloned.1.call-done = bf16[64,1536]{1,0:T(8,128)(2,1)} async-done(((bf16[1024,1536]{1,0:T(8,128)(2,1)}), bf16[64,1536]{1,0:T(8,128)(2,1)}) %reduce-scatter.6.cloned.1.call-update) | async-done | bytes 196624 | tf_op jit(solution)/shard_map/reduce_scatter | solution.py:313
  (378 shorter events, 155.1 us)
Async XLA Ops:
  7.2 58.4 %all-gather.5.cloned.1.call-start = ((), (), s32[]{:S(2)}) async-start(), calls=%async_computation.3 | async-start | bytes 4734976 | tf_op jit(solution)/shard_map/all_gather | solution.py:295
  10.6 107.0 %all-gather.7.cloned.1.call-start = ((), (), s32[]{:S(2)}) async-start(), calls=%async_computation.4 | async-start | bytes 4456448 | tf_op jit(solution)/shard_map/all_gather | solution.py:295
  12.4 156.5 %all-gather.9.cloned.1.call-start = ((), (), s32[]{:S(2)}) async-start(), calls=%async_computation.5 | async-start | bytes 4456448 | tf_op jit(solution)/shard_map/all_gather | solution.py:295
  16.2 20.5 %collective-permute-start.2 = (bf16[1024,1024]{0,1:T(8,128)(2,1)}, bf16[1024,1024]{0,1:T(8,128)(2,1)}, u32[]{:S(2)}, u32[]{:S(2)}) collective-permute-start(bf16[1024,1024]{0,1:T(8,128)(2,1)} %pad_maximum_fusion), channel_id=1, source_target_pairs={{1,2},{2,1},{5,6},{6,5},{9,10},{10,9},{13,14},{14,13},{17,18},{18,... | collective-permute-start | bytes 6291464 | tf_op jit(solution)/shard_map/ppermute | solution.py:274
  19.6 15.3 %collective-permute-start = (bf16[512,1024]{0,1:T(8,128)(2,1)S(1)}, bf16[512,1024]{0,1:T(8,128)(2,1)S(1)}, u32[]{:S(2)}, u32[]{:S(2)}) collective-permute-start(bf16[512,1024]{0,1:T(8,128)(2,1)S(1)} %copy.93), channel_id=1, source_target_pairs={{1,2},{2,1},{5,6},{6,5},{9,10},{10,9},{13,14},{14,13},{17,18},{18,... | collective-permute-start | bytes 3145736 | tf_op jit(solution)/shard_map/ppermute | solution.py:274
  20.4 8.6 %collective-permute-start.3 = (bf16[64,2048]{1,0:T(8,128)(2,1)S(1)}, bf16[64,2048]{1,0:T(8,128)(2,1)S(1)}, u32[]{:S(2)}, u32[]{:S(2)}) collective-permute-start(bf16[64,2048]{1,0:T(8,128)(2,1)S(1)} %copy-done.59), channel_id=1, source_target_pairs={{1,2},{2,1},{5,6},{6,5},{9,10},{10,9},{13,14},{14,13},{17,18},{18,... | collective-permute-start | bytes 786440 | tf_op jit(solution)/shard_map/ppermute | solution.py:274
  21.1 13.9 %collective-permute-start.4 = (bf16[64,2048]{1,0:T(8,128)(2,1)S(1)}, bf16[64,2048]{1,0:T(8,128)(2,1)S(1)}, u32[]{:S(2)}, u32[]{:S(2)}) collective-permute-start(bf16[64,2048]{1,0:T(8,128)(2,1)S(1)} %copy-done.59), channel_id=1, source_target_pairs={{0,1},{1,3},{3,2},{2,0},{4,5},{5,7},{7,6},{6,4},{8,9},{9,11},{11,1... | collective-permute-start | bytes 786440 | tf_op jit(solution)/shard_map/ppermute | solution.py:274
  28.3 0.7 collective-permute-start.1
  65.6 52.0 %collective-permute-start.6 = (bf16[1024,2176]{1,0:T(8,128)(2,1)}, bf16[1024,2176]{1,0:T(8,128)(2,1)}, u32[]{:S(2)}, u32[]{:S(2)}) collective-permute-start(bf16[1024,2176]{1,0:T(8,128)(2,1)} %all-gather.5.cloned.1.call-done), channel_id=1, source_target_pairs={{1,2},{2,1},{5,6},{6,5},{9,10},{10,9},{13,14},{14,13},{17,18},{18,... | collective-permute-start | bytes 13369352 | tf_op jit(solution)/shard_map/ppermute | solution.py:274
  68.4 174.4 %all-gather.11.cloned.1.call-start = ((), (), s32[]{:S(2)}) async-start(), calls=%async_computation.6 | async-start | bytes 4718592 | tf_op jit(solution)/shard_map/all_gather | solution.py:310
  69.9 8.5 %collective-permute-start.5 = (bf16[512,1024]{0,1:T(8,128)(2,1)}, bf16[512,1024]{0,1:T(8,128)(2,1)}, u32[]{:S(2)}, u32[]{:S(2)}) collective-permute-start(bf16[512,1024]{0,1:T(8,128)(2,1)} %broadcast_select_fusion.19), channel_id=1, source_target_pairs={{0,2},{1,3},{2,0},{3,1},{4,6},{5,7},{6,4},{7,5},{8,10},{9,11},{10,... | collective-permute-start | bytes 3145736 | tf_op jit(solution)/shard_map/ppermute | solution.py:274
  73.8 4.3 collective-permute-start.7
  75.9 72.8 %collective-permute-start.8 = (bf16[512,1024]{0,1:T(8,128)(2,1)}, bf16[512,1024]{0,1:T(8,128)(2,1)}, u32[]{:S(2)}, u32[]{:S(2)}) collective-permute-start(bf16[512,1024]{0,1:T(8,128)(2,1)} %slice.227), channel_id=1, source_target_pairs={{0,2},{1,3},{2,0},{3,1},{4,6},{5,7},{6,4},{7,5},{8,10},{9,11},{10,... | collective-permute-start | bytes 3145736 | tf_op jit(solution)/shard_map/ppermute | solution.py:274
  81.1 44.5 %copy-start.64 = (f32[1024]{0:T(1024)}, f32[1024]{0:T(1024)S(1)}, u32[]{:S(2)}) copy-start(f32[1024]{0:T(1024)S(1)} %broadcast_multiply_fusion.6) | copy-start | bytes 12292
  117.6 54.1 %collective-permute-start.10 = (bf16[1024,2048]{1,0:T(8,128)(2,1)}, bf16[1024,2048]{1,0:T(8,128)(2,1)}, u32[]{:S(2)}, u32[]{:S(2)}) collective-permute-start(bf16[1024,2048]{1,0:T(8,128)(2,1)} %all-gather.7.cloned.1.call-done), channel_id=1, source_target_pairs={{1,2},{2,1},{5,6},{6,5},{9,10},{10,9},{13,14},{14,13},{17,18},{18,... | collective-permute-start | bytes 12582920 | tf_op jit(solution)/shard_map/ppermute | solution.py:274
  144.3 206.0 %copy-start.4 = (bf16[1024,512]{1,0:T(8,128)(2,1)}, bf16[1024,512]{1,0:T(8,128)(2,1)S(1)}, u32[]{:S(2)}) copy-start(bf16[1024,512]{1,0:T(8,128)(2,1)S(1)} %get-tuple-element.73.refs_3_) | copy-start | bytes 3145732
  146.9 11.1 %collective-permute-start.9 = (bf16[1024,1024]{0,1:T(8,128)(2,1)}, bf16[1024,1024]{0,1:T(8,128)(2,1)}, u32[]{:S(2)}, u32[]{:S(2)}) collective-permute-start(bf16[1024,1024]{0,1:T(8,128)(2,1)} %fusion.47), channel_id=1, source_target_pairs={{0,2},{1,3},{2,0},{3,1},{4,6},{5,7},{6,4},{7,5},{8,10},{9,11},{10,... | collective-permute-start | bytes 6291464 | tf_op jit(solution)/shard_map/ppermute | solution.py:274
  151.8 3.2 collective-permute-start.11
  153.3 179.1 %reduce-scatter.4.cloned.1.call-start = ((), (), s32[]{:S(2)}) async-start(), calls=%async_computation.7 | async-start | bytes 4718592 | tf_op jit(solution)/shard_map/reduce_scatter | solution.py:316
  168.9 40.9 %collective-permute-start.13 = (bf16[1024,2048]{1,0:T(8,128)(2,1)}, bf16[1024,2048]{1,0:T(8,128)(2,1)}, u32[]{:S(2)}, u32[]{:S(2)}) collective-permute-start(bf16[1024,2048]{1,0:T(8,128)(2,1)} %all-gather.9.cloned.1.call-done), channel_id=1, source_target_pairs={{1,2},{2,1},{5,6},{6,5},{9,10},{10,9},{13,14},{14,13},{17,18},{18,... | collective-permute-start | bytes 12582920 | tf_op jit(solution)/shard_map/ppermute | solution.py:274
  198.0 4.9 collective-permute-start.12
  242.8 274.3 %reduce-scatter.8.cloned.1.call-start = ((), (), s32[]{:S(2)}) async-start(), calls=%async_computation.9 | async-start | bytes 4456448 | tf_op jit(solution)/shard_map/reduce_scatter | solution.py:313
  256.4 12.8 %collective-permute-start.14 = (bf16[1024,1024]{0,1:T(8,128)(2,1)S(1)}, bf16[1024,1024]{0,1:T(8,128)(2,1)S(1)}, u32[]{:S(2)}, u32[]{:S(2)}) collective-permute-start(bf16[1024,1024]{0,1:T(8,128)(2,1)S(1)} %fusion.26), channel_id=1, source_target_pairs={{0,2},{1,3},{2,0},{3,1},{4,6},{5,7},{6,4},{7,5},{8,10},{9,11},{10,... | collective-permute-start | bytes 6291464 | tf_op jit(solution)/shard_map/ppermute | solution.py:274
  266.4 58.6 %collective-permute-start.16 = (bf16[1024,2048]{1,0:T(8,128)(2,1)}, bf16[1024,2048]{1,0:T(8,128)(2,1)}, u32[]{:S(2)}, u32[]{:S(2)}) collective-permute-start(bf16[1024,2048]{1,0:T(8,128)(2,1)} %fusion.72), channel_id=1, source_target_pairs={{1,2},{2,1},{5,6},{6,5},{9,10},{10,9},{13,14},{14,13},{17,18},{18,... | collective-permute-start | bytes 12582920 | tf_op jit(solution)/shard_map/ppermute | solution.py:274
  311.1 27.3 %collective-permute-start.15 = (bf16[1024,1024]{0,1:T(8,128)(2,1)}, bf16[1024,1024]{0,1:T(8,128)(2,1)}, u32[]{:S(2)}, u32[]{:S(2)}) collective-permute-start(bf16[1024,1024]{0,1:T(8,128)(2,1)} %fusion.42), channel_id=1, source_target_pairs={{0,2},{1,3},{2,0},{3,1},{4,6},{5,7},{6,4},{7,5},{8,10},{9,11},{10,... | collective-permute-start | bytes 6291464 | tf_op jit(solution)/shard_map/ppermute | solution.py:274
  356.2 169.4 %reduce-scatter.6.cloned.1.call-start = ((), (), s32[]{:S(2)}) async-start(), calls=%async_computation.8 | async-start | bytes 3342336 | tf_op jit(solution)/shard_map/reduce_scatter | solution.py:313
  358.6 39.4 %collective-permute-start.18 = (bf16[2,2,2,64,1280]{4,3,1,0,2:T(8,128)(2,1)S(1)}, bf16[2,2,2,64,1280]{4,3,1,0,2:T(8,128)(2,1)S(1)}, u32[]{:S(2)}, u32[]{:S(2)}) collective-permute-start(bf16[2,2,2,64,1280]{4,3,1,0,2:T(8,128)(2,1)S(1)} %pad_maximum_fusion.6), channel_id=1, source_target_pairs={{1,2},{2,1},{5,6},{6,5},{9,10},{10,9},{13,14},{14,13},{17,18},{18,... | collective-permute-start | bytes 3932168 | tf_op jit(solution)/shard_map/ppermute | solution.py:274
  359.6 38.4 %collective-permute-start.20 = (bf16[2,2,2,64,1280]{4,3,2,1,0:T(8,128)(2,1)S(1)}, bf16[2,2,2,64,1280]{4,3,2,1,0:T(8,128)(2,1)S(1)}, u32[]{:S(2)}, u32[]{:S(2)}) collective-permute-start(bf16[2,2,2,64,1280]{4,3,2,1,0:T(8,128)(2,1)S(1)} %pad_maximum_fusion.8), channel_id=1, source_target_pairs={{0,4},{1,5},{2,6},{3,7},{4,0},{5,1},{6,2},{7,3},{8,12},{9,13},{10,... | collective-permute-start | bytes 3932168 | tf_op jit(solution)/shard_map/ppermute | solution.py:274
  361.2 36.7 %collective-permute-start.19 = (bf16[2,2,2,64,1280]{4,3,1,0,2:T(8,128)(2,1)S(1)}, bf16[2,2,2,64,1280]{4,3,1,0,2:T(8,128)(2,1)S(1)}, u32[]{:S(2)}, u32[]{:S(2)}) collective-permute-start(bf16[2,2,2,64,1280]{4,3,1,0,2:T(8,128)(2,1)S(1)} %pad_maximum_fusion.7), channel_id=1, source_target_pairs={{1,0},{3,1},{2,3},{0,2},{5,4},{7,5},{6,7},{4,6},{9,8},{11,9},{10,1... | collective-permute-start | bytes 3932168 | tf_op jit(solution)/shard_map/ppermute | solution.py:274
  389.7 28.9 %collective-permute-start.17 = (bf16[1024,1536]{1,0:T(8,128)(2,1)}, bf16[1024,1536]{1,0:T(8,128)(2,1)}, u32[]{:S(2)}, u32[]{:S(2)}) collective-permute-start(bf16[1024,1536]{1,0:T(8,128)(2,1)} %fusion.62), channel_id=1, source_target_pairs={{1,2},{2,1},{5,6},{6,5},{9,10},{10,9},{13,14},{14,13},{17,18},{18,... | collective-permute-start | bytes 9437192 | tf_op jit(solution)/shard_map/ppermute | solution.py:274
  399.5 36.8 %collective-permute-start.26 = (bf16[2,2,64,1280]{3,2,1,0:T(8,128)(2,1)}, bf16[2,2,64,1280]{3,2,1,0:T(8,128)(2,1)}, u32[]{:S(2)}, u32[]{:S(2)}) collective-permute-start(bf16[2,2,64,1280]{3,2,1,0:T(8,128)(2,1)} %dynamic-slice_bitcast_fusion.4), channel_id=1, source_target_pairs={{0,4},{1,5},{2,6},{3,7},{4,0},{5,1},{6,2},{7,3},{8,12},{9,13},{10,... | collective-permute-start | bytes 1966088 | tf_op jit(solution)/shard_map/ppermute | solution.py:274
  401.5 35.0 %collective-permute-start.28 = (bf16[2,2,64,1280]{3,2,1,0:T(8,128)(2,1)}, bf16[2,2,64,1280]{3,2,1,0:T(8,128)(2,1)}, u32[]{:S(2)}, u32[]{:S(2)}) collective-permute-start(bf16[2,2,64,1280]{3,2,1,0:T(8,128)(2,1)} %get-tuple-element.206), channel_id=1, source_target_pairs={{1,0},{3,1},{2,3},{0,2},{5,4},{7,5},{6,7},{4,6},{9,8},{11,9},{10,1... | collective-permute-start | bytes 1966088 | tf_op jit(solution)/shard_map/ppermute | solution.py:274
  401.5 36.5 %collective-permute-start.27 = (bf16[2,2,64,1280]{3,2,1,0:T(8,128)(2,1)S(1)}, bf16[2,2,64,1280]{3,2,1,0:T(8,128)(2,1)}, u32[]{:S(2)}, u32[]{:S(2)}) collective-permute-start(bf16[2,2,64,1280]{3,2,1,0:T(8,128)(2,1)S(1)} %get-tuple-element.207), channel_id=1, source_target_pairs={{1,2},{2,1},{5,6},{6,5},{9,10},{10,9},{13,14},{14,13},{17,18},{18,... | collective-permute-start | bytes 1966088 | tf_op jit(solution)/shard_map/ppermute | solution.py:274
  424.2 20.9 %collective-permute-start.21 = (bf16[512,1024]{0,1:T(8,128)(2,1)S(1)}, bf16[512,1024]{0,1:T(8,128)(2,1)S(1)}, u32[]{:S(2)}, u32[]{:S(2)}) collective-permute-start(bf16[512,1024]{0,1:T(8,128)(2,1)S(1)} %broadcast_select_fusion.8), channel_id=1, source_target_pairs={{0,2},{1,3},{2,0},{3,1},{4,6},{5,7},{6,4},{7,5},{8,10},{9,11},{10,... | collective-permute-start | bytes 3145736 | tf_op jit(solution)/shard_map/ppermute | solution.py:274
  434.8 13.9 %collective-permute-start.23 = (bf16[512,1024]{0,1:T(8,128)(2,1)S(1)}, bf16[512,1024]{0,1:T(8,128)(2,1)S(1)}, u32[]{:S(2)}, u32[]{:S(2)}) collective-permute-start(bf16[512,1024]{0,1:T(8,128)(2,1)S(1)} %broadcast_select_fusion.9), channel_id=1, source_target_pairs={{0,2},{1,3},{2,0},{3,1},{4,6},{5,7},{6,4},{7,5},{8,10},{9,11},{10,... | collective-permute-start | bytes 3145736 | tf_op jit(solution)/shard_map/ppermute | solution.py:274
  436.3 53.1 %collective-permute-start.31 = (bf16[64,2048]{1,0:T(8,128)(2,1)S(1)}, bf16[64,2048]{1,0:T(8,128)(2,1)}, u32[]{:S(2)}, u32[]{:S(2)}) collective-permute-start(bf16[64,2048]{1,0:T(8,128)(2,1)S(1)} %copy-done.58), channel_id=1, source_target_pairs={{1,0},{3,1},{2,3},{0,2},{5,4},{7,5},{6,7},{4,6},{9,8},{11,9},{10,1... | collective-permute-start | bytes 786440 | tf_op jit(solution)/shard_map/ppermute | solution.py:274
  436.5 52.9 %collective-permute-start.30 = (bf16[64,2048]{1,0:T(8,128)(2,1)S(1)}, bf16[64,2048]{1,0:T(8,128)(2,1)}, u32[]{:S(2)}, u32[]{:S(2)}) collective-permute-start(bf16[64,2048]{1,0:T(8,128)(2,1)S(1)} %get-tuple-element.223), channel_id=1, source_target_pairs={{1,2},{2,1},{5,6},{6,5},{9,10},{10,9},{13,14},{14,13},{17,18},{18,... | collective-permute-start | bytes 786440 | tf_op jit(solution)/shard_map/ppermute | solution.py:274
  438.0 18.3 %collective-permute-start.25 = (bf16[512,1024]{0,1:T(8,128)(2,1)}, bf16[512,1024]{0,1:T(8,128)(2,1)}, u32[]{:S(2)}, u32[]{:S(2)}) collective-permute-start(bf16[512,1024]{0,1:T(8,128)(2,1)} %broadcast_select_fusion.10), channel_id=1, source_target_pairs={{0,2},{1,3},{2,0},{3,1},{4,6},{5,7},{6,4},{7,5},{8,10},{9,11},{10,... | collective-permute-start | bytes 3145736 | tf_op jit(solution)/shard_map/ppermute | solution.py:274
  446.9 15.7 %collective-permute-start.22 = (bf16[512,1024]{0,1:T(8,128)(2,1)}, bf16[512,1024]{0,1:T(8,128)(2,1)}, u32[]{:S(2)}, u32[]{:S(2)}) collective-permute-start(bf16[512,1024]{0,1:T(8,128)(2,1)} %fusion.18), channel_id=1, source_target_pairs={{1,2},{2,1},{5,6},{6,5},{9,10},{10,9},{13,14},{14,13},{17,18},{18,... | collective-permute-start | bytes 3145736 | tf_op jit(solution)/shard_map/ppermute | solution.py:274
  450.1 12.5 %collective-permute-start.24 = (bf16[512,1024]{0,1:T(8,128)(2,1)}, bf16[512,1024]{0,1:T(8,128)(2,1)}, u32[]{:S(2)}, u32[]{:S(2)}) collective-permute-start(bf16[512,1024]{0,1:T(8,128)(2,1)} %add_convert_fusion.5), channel_id=1, source_target_pairs={{1,2},{2,1},{5,6},{6,5},{9,10},{10,9},{13,14},{14,13},{17,18},{18,... | collective-permute-start | bytes 3145736 | tf_op jit(solution)/shard_map/ppermute | solution.py:274
  456.2 35.2 %collective-permute-start.29 = (bf16[2,64,2560]{2,1,0:T(8,128)(2,1)}, bf16[2,64,2560]{2,1,0:T(8,128)(2,1)}, u32[]{:S(2)}, u32[]{:S(2)}) collective-permute-start(bf16[2,64,2560]{2,1,0:T(8,128)(2,1)} %fusion.50), channel_id=1, source_target_pairs={{0,16},{1,17},{2,18},{3,19},{4,20},{5,21},{6,22},{7,23},{8,24},{9,... | collective-permute-start | bytes 1966088 | tf_op jit(solution)/shard_map/ppermute | solution.py:274
  462.6 18.9 %collective-permute-start.32 = (f32[8,1024]{1,0:T(8,128)S(1)}, f32[8,1024]{1,0:T(8,128)S(1)}, u32[]{:S(2)}, u32[]{:S(2)}) collective-permute-start(f32[8,1024]{1,0:T(8,128)S(1)} %stack.31), channel_id=1, source_target_pairs={{0,2},{1,3},{2,0},{3,1},{4,6},{5,7},{6,4},{7,5},{8,10},{9,11},{10,... | collective-permute-start | bytes 98312 | tf_op jit(solution)/shard_map/ppermute | solution.py:274
  479.8 27.2 %collective-permute-start.35 = (bf16[512,1024]{0,1:T(8,128)(2,1)}, bf16[512,1024]{0,1:T(8,128)(2,1)}, u32[]{:S(2)}, u32[]{:S(2)}) collective-permute-start(bf16[512,1024]{0,1:T(8,128)(2,1)} %fusion.12), channel_id=1, source_target_pairs={{1,2},{2,1},{5,6},{6,5},{9,10},{10,9},{13,14},{14,13},{17,18},{18,... | collective-permute-start | bytes 3145736 | tf_op jit(solution)/shard_map/ppermute | solution.py:274
  481.5 7.9 %collective-permute-start.33 = (f32[8,1024]{1,0:T(8,128)S(1)}, f32[8,1024]{1,0:T(8,128)S(1)}, u32[]{:S(2)}, u32[]{:S(2)}) collective-permute-start(f32[8,1024]{1,0:T(8,128)S(1)} %add.264), channel_id=1, source_target_pairs={{0,4},{1,5},{2,6},{3,7},{4,0},{5,1},{6,2},{7,3},{8,12},{9,13},{10,... | collective-permute-start | bytes 98312 | tf_op jit(solution)/shard_map/ppermute | solution.py:274
  491.4 5.3 collective-permute-start.36
  496.7 6.0 %collective-permute-start.37 = (f32[8,1024]{1,0:T(8,128)S(1)}, f32[8,1024]{1,0:T(8,128)S(1)}, u32[]{:S(2)}, u32[]{:S(2)}) collective-permute-start(f32[8,1024]{1,0:T(8,128)S(1)} %add.269), channel_id=1, source_target_pairs={{0,16},{1,17},{2,18},{3,19},{4,20},{5,21},{6,22},{7,23},{8,24},{9,... | collective-permute-start | bytes 98312 | tf_op jit(solution)/shard_map/ppermute | solution.py:274
  498.5 12.2 %collective-permute-start.34 = (bf16[64,2560]{1,0:T(8,128)(2,1)S(1)}, bf16[64,2560]{1,0:T(8,128)(2,1)S(1)}, u32[]{:S(2)}, u32[]{:S(2)}) collective-permute-start(bf16[64,2560]{1,0:T(8,128)(2,1)S(1)} %dynamic-slice_bitcast_fusion.5), channel_id=1, source_target_pairs={{0,8},{1,9},{2,10},{3,11},{4,12},{5,13},{6,14},{7,15},{8,0},{9,1},... | collective-permute-start | bytes 983048 | tf_op jit(solution)/shard_map/ppermute | solution.py:274
  502.7 4.2 collective-permute-start.38
  (79 other events, 515.3 us)
Sparse Core Ops, SparseCore 0:
  10.9 54.6 all-gather.4
  68.3 49.2 all-gather.6
  119.8 49.0 all-gather.8
  170.8 71.8 all-gather.10
  246.2 86.1 reduce-scatter.3
  356.3 76.8 reduce-scatter.7
  454.5 71.0 reduce-scatter.5
